TPU v7x, 128 devices: a whole 4x4x4 slice. The times are simulated.
128 devices in a mesh: qgrp: 16 (over z, x), pcol: 8 (over y, core).
Axes of the slice: x: 4, y: 4, z: 4, core: 2. Of those that a mesh axis runs over, the one named last changes fastest.
Arguments:
- queries: bfloat16 [16384, 1024], P('qgrp'), may hold values from -80 to 80
- passages: bfloat16 [131072, 1024], P(('qgrp', 'pcol')), may hold values from -1.5 to 1.5
- block_mask: int32 [2, 16], replicated, may hold values 0 or 1
- positives: int32 [16384], P('qgrp'), may hold values from 0 to 8191
Outputs:
- query_loss: float32 [16384], P('qgrp')
- query_grad: bfloat16 [16384, 1024], P(('qgrp', 'pcol'))
- passage_grad: bfloat16 [131072, 1024], P(('qgrp', 'pcol'))
All inputs are finite; a program needn't handle non-finite values.
Results may differ from a plain program's by a relative error of at most 0.017.
Values may be sent and summed in bfloat16 or wider, within the bound.
A program may use at most 128 MiB of HBM per device.

v0:
```python
import jax
import jax.numpy as jnp
from jax import lax
from jax.sharding import PartitionSpec as P

ROUNDS = 2


minus_inf = -jnp.inf


def partner(value, axis, distance):
    mask = 2**distance
    pairs = [(source, source ^ mask) for source in range(lax.axis_size(axis))]
    return lax.ppermute(value, axis, pairs)


def block_stats(logits):
    peak = jnp.max(logits, axis=1)
    return (peak, jnp.sum(jnp.exp(logits - peak[:, None]), axis=1))


def mask_flag(block_mask, round_index, group_index):
    return lax.dynamic_index_in_dim(block_mask[round_index], group_index, 0, keepdims=False) > 0


def on_device(queries, passages, block_mask, positives):
    shard_rows = passages.shape[0]
    column_start = lax.axis_index("pcol") * shard_rows
    group_index = lax.axis_index("qgrp")
    keep_flags = [mask_flag(block_mask, round_index, group_index) for round_index in range(ROUNDS)]
    own_logits = jnp.einsum("qd,pd->qp", queries, passages, preferred_element_type=jnp.float32)
    stats_list = [block_stats(own_logits)]
    lent_blocks = []
    for round_index in range(ROUNDS):
        lent_blocks.append(partner(passages, "qgrp", round_index))
    round_logits = [
        jnp.einsum("qd,pd->qp", queries, block_rows, preferred_element_type=jnp.float32)
        for block_rows in lent_blocks
    ]
    for logits_round in round_logits:
        stats_list.append(block_stats(logits_round))
    local_maximum = stats_list[0][0]
    for stats_round, flag_round in zip(stats_list[1:], keep_flags):
        local_maximum = jnp.maximum(local_maximum, jnp.where(flag_round, stats_round[0], minus_inf))
    local_sum = stats_list[0][1] * jnp.exp(stats_list[0][0] - local_maximum)
    for stats_round, flag_round in zip(stats_list[1:], keep_flags):
        local_sum = local_sum + jnp.where(
            flag_round, stats_round[1] * jnp.exp(stats_round[0] - local_maximum), 0.0
        )
    is_positive = (
        lax.broadcasted_iota(jnp.int32, (1, shard_rows), 1) + column_start == positives[:, None]
    )
    positive_part = jnp.sum(jnp.where(is_positive, own_logits, 0.0), axis=1)
    row_maximum = lax.pmax(local_maximum, "pcol")
    exp_total, positive_logit = lax.psum(
        (local_sum * jnp.exp(local_maximum - row_maximum), positive_part), "pcol"
    )
    log_total = row_maximum + jnp.log(exp_total)
    query_loss = log_total - positive_logit
    own_weights = (
        jnp.exp(own_logits - log_total[:, None]) - is_positive.astype(jnp.float32)
    ).astype(jnp.bfloat16)
    passage_grad = jnp.einsum("qp,qd->pd", own_weights, queries, preferred_element_type=jnp.float32)
    round_weights = [
        jnp.where(flag_round, jnp.exp(logits_round - log_total[:, None]), 0.0).astype(jnp.bfloat16)
        for logits_round, flag_round in zip(round_logits, keep_flags)
    ]
    for round_index in range(ROUNDS):
        lent_grad = jnp.einsum(
            "qp,qd->pd", round_weights[round_index], queries, preferred_element_type=jnp.float32
        )
        passage_grad = passage_grad + partner(
            lent_grad.astype(jnp.bfloat16), "qgrp", round_index
        ).astype(lent_grad.dtype)
    term_sum = jnp.dot(own_weights, passages, preferred_element_type=jnp.float32)
    for weights_round, block_rows in zip(round_weights, lent_blocks):
        term_sum = term_sum + jnp.dot(weights_round, block_rows, preferred_element_type=jnp.float32)
    query_grad = lax.psum_scatter(
        term_sum.astype(jnp.bfloat16), "pcol", scatter_dimension=0, tiled=True
    )
    return (query_loss, query_grad, passage_grad.astype(jnp.bfloat16))


def solution(mesh):
    in_specs = (P("qgrp", None), P(("qgrp", "pcol"), None), P(), P("qgrp"))
    out_specs = (P("qgrp"), P(("qgrp", "pcol"), None), P(("qgrp", "pcol"), None))
    return jax.shard_map(
        on_device, mesh=mesh, in_specs=in_specs, out_specs=out_specs, check_vma=False
    )
```

profile of v0, /device:TPU:24, one launch (start us, length us, event | category | flops | bytes accessed | tf_op | source)
XLA Modules:
  0.0 267.4 jit_solution(16279030527928335559)
XLA Ops:
  7.2 3.1 %collective-permute-start.1 = (bf16[1024,1024]{1,0:T(8,128)(2,1)}, bf16[1024,1024]{1,0:T(8,128)(2,1)}, u32[]{:S(2)}, u32[]{:S(2)}) collective-permute-start(bf16[1024,1024]{1,0:T(8,128)(2,1)} %param.5), channel_id=1, source_target_pairs={{0,16},{8,24},{16,0},{24,8},{32,48},{40,56},{48,32},{56,40},{64,80... | collective-permute-start | bytes 6291464 | tf_op jit(solution)/shard_map/ppermute | solution.py:15
  10.9 0.8 fusion.15
  12.3 4.0 %fusion.17 = (f32[1024]{0:T(1024)S(1)}, f32[1024,1024]{0,1:T(8,128)S(1)}) fusion(bf16[1024,1024]{1,0:T(8,128)(2,1)S(1)} %copy-done, bf16[1024,1024]{1,0:T(8,128)(2,1)} %param.5), kind=kOutput, calls=%fused_computation.30 | convolution fusion | flops 2148531200 | bytes 8392704 | tf_op jit(solution)/shard_map/qd,pd->qp/dot_general | solution.py:32
  16.3 1.4 fusion
  17.7 39.9 %collective-permute-done.1 = bf16[1024,1024]{1,0:T(8,128)(2,1)} collective-permute-done((bf16[1024,1024]{1,0:T(8,128)(2,1)}, bf16[1024,1024]{1,0:T(8,128)(2,1)}, u32[]{:S(2)}, u32[]{:S(2)}) %collective-permute-start.1) | collective-permute-done | bytes 2097184 | tf_op jit(solution)/shard_map/ppermute | solution.py:15
  57.6 5.9 %fusion.16 = (f32[1024]{0:T(1024)S(1)}, f32[1024,1024]{0,1:T(8,128)}) fusion(bf16[1024,1024]{1,0:T(8,128)(2,1)S(1)} %copy-done, bf16[1024,1024]{1,0:T(8,128)(2,1)} %collective-permute-done.1), kind=kOutput, calls=%fused_computation.29 | convolution fusion | flops 2148531200 | bytes 8392704 | tf_op jit(solution)/shard_map/qd,pd->qp/dot_general | solution.py:38
  63.6 37.9 %collective-permute-done = bf16[1024,1024]{1,0:T(8,128)(2,1)} collective-permute-done((bf16[1024,1024]{1,0:T(8,128)(2,1)}, bf16[1024,1024]{1,0:T(8,128)(2,1)}, u32[]{:S(2)}, u32[]{:S(2)}) %collective-permute-start) | collective-permute-done | bytes 2097184 | tf_op jit(solution)/shard_map/ppermute | solution.py:15
  101.5 5.9 %fusion.18 = (f32[1024]{0:T(1024)S(1)}, f32[1024,1024]{0,1:T(8,128)}) fusion(bf16[1024,1024]{1,0:T(8,128)(2,1)S(1)} %copy-done, bf16[1024,1024]{1,0:T(8,128)(2,1)} %collective-permute-done), kind=kOutput, calls=%fused_computation.31 | convolution fusion | flops 2148531200 | bytes 8392704 | tf_op jit(solution)/shard_map/qd,pd->qp/dot_general | solution.py:38
  107.5 1.2 select_maximum_fusion
  108.7 10.0 %pmax.7 = f32[1024]{0:T(1024)S(1)} all-reduce(f32[1024]{0:T(1024)S(1)} %select_maximum_fusion), channel_id=1, replica_groups=mesh['qgrp'=16,'pcol'=8] {'pcol'}, use_global_device_ids=true, to_apply=%region_3.4 | all-reduce | flops 1024 | bytes 8192 | tf_op jit(solution)/shard_map/pmax | solution.py:55
  118.7 3.0 %exponential_reduce_fusion = f32[1024]{0:T(1024)S(1)} fusion(f32[1024,1024]{0,1:T(8,128)} %get-tuple-element.12, f32[1024]{0:T(1024)S(1)} %get-tuple-element.11), kind=kLoop, calls=%fused_computation.9 | loop fusion | flops 2096128 | bytes 4202496 | tf_op jit(solution)/shard_map/reduce_sum | solution.py:20
  122.1 0.6 exponential_reduce_fusion.1
  122.8 1.2 exponential_multiply_fusion
  124.0 13.0 %all-reduce = (f32[1024]{0:T(1024)S(1)}, f32[1024]{0:T(1024)S(1)}) all-reduce(f32[1024]{0:T(1024)S(1)} %exponential_multiply_fusion, f32[1024]{0:T(1024)S(1)} %get-tuple-element.3), channel_id=1, replica_groups=mesh['qgrp'=16,'pcol'=8] {'pcol'}, use_global_device_ids=true, to_apply=%region_7.8 | all-reduce | flops 2048 | bytes 16384 | tf_op jit(solution)/shard_map/psum | solution.py:56
  137.6 5.6 %fusion.10 = f32[1024,1024]{1,0:T(8,128)S(1)} fusion(bf16[1024,1024]{1,0:T(8,128)(2,1)} %param.5, f32[1024,1024]{0,1:T(8,128)} %copy-done.1, f32[1024]{0:T(1024)S(1)} %get-tuple-element.8, s32[1024]{0:T(1024)S(1)} %copy-done.7, s32[1024]{0:T(1024)S(1)} %iota_add_fusion), kind=kOutput, calls=%fused_computation.26 | convolution fusion | flops 2152726528 | bytes 10498048 | tf_op jit(solution)/shard_map/dot_general | solution.py:76
  143.2 4.9 %fusion.3 = f32[1024,1024]{1,0:T(8,128)S(1)} fusion(bf16[1024,1024]{1,0:T(8,128)(2,1)} %collective-permute-done, f32[1024,1024]{0,1:T(8,128)S(1)} %copy-done.6, f32[1024]{0:T(1024)S(1)} %get-tuple-element.8, pred[]{:T(512)} %bitcast), kind=kOutput, calls=%fused_computation.14 | convolution fusion | flops 2150629376 | bytes 10489857 | tf_op jit(solution)/shard_map/dot_general | solution.py:78
  148.1 6.3 %add_convert_fusion.1 = bf16[1024,1024]{1,0:T(8,128)(2,1)} fusion(f32[1024,1024]{1,0:T(8,128)S(1)} %fusion.10, f32[1024,1024]{1,0:T(8,128)S(1)} %fusion.3, bf16[1024,1024]{1,0:T(8,128)(2,1)} %collective-permute-done.1, f32[1024,1024]{0,1:T(8,128)S(1)} %copy-done.3, f32[1024]{0:T(1024)S(1)} %get-tuple-element.8, pred[]{:T(512)} %bitcast.1), kind=kOutput, calls=%fused_computation.6 | convolution fusion | flops 2153775104 | bytes 16781312 | tf_op jit(solution)/shard_map/dot_general | solution.py:78
  154.5 5.4 %convolution_convert_fusion.1 = bf16[1024,1024]{1,0:T(8,128)(2,1)S(1)} fusion(bf16[1024,1024]{1,0:T(8,128)(2,1)S(1)} %copy-done, f32[1024,1024]{0,1:T(8,128)} %get-tuple-element.16, f32[1024]{0:T(1024)S(1)} %get-tuple-element.8, pred[]{:T(512)} %bitcast), kind=kOutput, calls=%fused_computation.13 | convolution fusion | flops 2151677952 | bytes 8392705 | tf_op jit(solution)/shard_map/qp,qd->pd/dot_general | solution.py:70
  159.8 3.2 %convolution_convert_fusion = bf16[1024,1024]{1,0:T(8,128)(2,1)S(1)} fusion(bf16[1024,1024]{1,0:T(8,128)(2,1)S(1)} %copy-done, f32[1024,1024]{0,1:T(8,128)S(1)} %copy-done.4, f32[1024]{0:T(1024)S(1)} %get-tuple-element.8, pred[]{:T(512)} %bitcast.1), kind=kOutput, calls=%fused_computation.12 | convolution fusion | flops 2151677952 | bytes 8392705 | tf_op jit(solution)/shard_map/qp,qd->pd/dot_general | solution.py:70
  163.0 1.5 collective-permute-start.2
  164.5 0.7 collective-permute-start.3
  165.2 46.4 %collective-permute-done.2 = bf16[1024,1024]{1,0:T(8,128)(2,1)S(1)} collective-permute-done((bf16[1024,1024]{1,0:T(8,128)(2,1)S(1)}, bf16[1024,1024]{1,0:T(8,128)(2,1)S(1)}, u32[]{:S(2)}, u32[]{:S(2)}) %collective-permute-start.2) | collective-permute-done | bytes 2097184 | tf_op jit(solution)/shard_map/ppermute | solution.py:15
  211.6 44.9 %collective-permute-done.3 = bf16[1024,1024]{1,0:T(8,128)(2,1)S(1)} collective-permute-done((bf16[1024,1024]{1,0:T(8,128)(2,1)S(1)}, bf16[1024,1024]{1,0:T(8,128)(2,1)S(1)}, u32[]{:S(2)}, u32[]{:S(2)}) %collective-permute-start.3) | collective-permute-done | bytes 2097184 | tf_op jit(solution)/shard_map/ppermute | solution.py:15
  256.5 4.0 %add_convert_fusion = bf16[1024,1024]{1,0:T(8,128)(2,1)} fusion(bf16[1024,1024]{1,0:T(8,128)(2,1)S(1)} %collective-permute-done.3, bf16[1024,1024]{1,0:T(8,128)(2,1)S(1)} %collective-permute-done.2, bf16[1024,1024]{1,0:T(8,128)(2,1)S(1)} %copy-done, f32[1024,1024]{0,1:T(8,128)S(1)} %copy-done.2, f32[1024]{0:T(1024)S(1)} %get-tuple-element.8, ...), kind=kOutput, calls=%fused_computation.5 | convolution fusion | flops 2157969408 | bytes 12595200 | tf_op jit(solution)/shard_map/qp,qd->pd/dot_general | solution.py:64
  (23 shorter events, 2.4 us)
Async XLA Ops:
  7.2 5.1 %copy-start = (bf16[1024,1024]{1,0:T(8,128)(2,1)S(1)}, bf16[1024,1024]{1,0:T(8,128)(2,1)}, u32[]{:S(2)}) copy-start(bf16[1024,1024]{1,0:T(8,128)(2,1)} %param.4) | copy-start | bytes 6291460
  7.2 253.3 %reduce-scatter.2.cloned.1.call-start = ((), (), s32[]{:S(2)}) async-start(), calls=%async_computation.1 | async-start | bytes 2359296 | tf_op jit(solution)/shard_map/reduce_scatter | solution.py:79
  7.2 50.4 %collective-permute-start.1 = (bf16[1024,1024]{1,0:T(8,128)(2,1)}, bf16[1024,1024]{1,0:T(8,128)(2,1)}, u32[]{:S(2)}, u32[]{:S(2)}) collective-permute-start(bf16[1024,1024]{1,0:T(8,128)(2,1)} %param.5), channel_id=1, source_target_pairs={{0,16},{8,24},{16,0},{24,8},{32,48},{40,56},{48,32},{56,40},{64,80... | collective-permute-start | bytes 6291464 | tf_op jit(solution)/shard_map/ppermute | solution.py:15
  10.3 91.2 %collective-permute-start = (bf16[1024,1024]{1,0:T(8,128)(2,1)}, bf16[1024,1024]{1,0:T(8,128)(2,1)}, u32[]{:S(2)}, u32[]{:S(2)}) collective-permute-start(bf16[1024,1024]{1,0:T(8,128)(2,1)} %param.5), channel_id=1, source_target_pairs={{0,8},{8,0},{16,24},{24,16},{32,40},{40,32},{48,56},{56,48},{64,72... | collective-permute-start | bytes 6291464 | tf_op jit(solution)/shard_map/ppermute | solution.py:15
  12.3 4.0 %copy-start.7 = (s32[1024]{0:T(1024)S(1)}, s32[1024]{0:T(1024)}, u32[]{:S(2)}) copy-start(s32[1024]{0:T(1024)} %param.7) | copy-start | bytes 12292
  16.3 47.3 %copy-start.1 = (f32[1024,1024]{0,1:T(8,128)}, f32[1024,1024]{0,1:T(8,128)S(1)}, u32[]{:S(2)}) copy-start(f32[1024,1024]{0,1:T(8,128)S(1)} %get-tuple-element.14) | copy-start | bytes 12582916
  118.7 3.4 %copy-start.5 = (f32[1024,1024]{0,1:T(8,128)S(1)}, f32[1024,1024]{0,1:T(8,128)}, u32[]{:S(2)}) copy-start(f32[1024,1024]{0,1:T(8,128)} %get-tuple-element.16) | copy-start | bytes 12582916
  137.6 5.6 %copy-start.6 = (f32[1024,1024]{0,1:T(8,128)S(1)}, f32[1024,1024]{0,1:T(8,128)}, u32[]{:S(2)}) copy-start(f32[1024,1024]{0,1:T(8,128)} %get-tuple-element.16) | copy-start | bytes 12582916
  143.2 4.9 %copy-start.3 = (f32[1024,1024]{0,1:T(8,128)S(1)}, f32[1024,1024]{0,1:T(8,128)}, u32[]{:S(2)}) copy-start(f32[1024,1024]{0,1:T(8,128)} %get-tuple-element.12) | copy-start | bytes 12582916
  154.4 5.4 %copy-start.4 = (f32[1024,1024]{0,1:T(8,128)S(1)}, f32[1024,1024]{0,1:T(8,128)}, u32[]{:S(2)}) copy-start(f32[1024,1024]{0,1:T(8,128)} %get-tuple-element.12) | copy-start | bytes 12582916
  159.8 96.7 %copy-start.2 = (f32[1024,1024]{0,1:T(8,128)S(1)}, f32[1024,1024]{0,1:T(8,128)}, u32[]{:S(2)}) copy-start(f32[1024,1024]{0,1:T(8,128)} %copy-done.1) | copy-start | bytes 12582916
  163.0 48.6 %collective-permute-start.2 = (bf16[1024,1024]{1,0:T(8,128)(2,1)S(1)}, bf16[1024,1024]{1,0:T(8,128)(2,1)S(1)}, u32[]{:S(2)}, u32[]{:S(2)}) collective-permute-start(bf16[1024,1024]{1,0:T(8,128)(2,1)S(1)} %convolution_convert_fusion.1), channel_id=1, source_target_pairs={{0,8},{8,0},{16,24},{24,16},{32,40},{40,32},{48,56},{56,48},{64,72... | collective-permute-start | bytes 6291464 | tf_op jit(solution)/shard_map/ppermute | solution.py:15
  164.5 92.0 %collective-permute-start.3 = (bf16[1024,1024]{1,0:T(8,128)(2,1)S(1)}, bf16[1024,1024]{1,0:T(8,128)(2,1)S(1)}, u32[]{:S(2)}, u32[]{:S(2)}) collective-permute-start(bf16[1024,1024]{1,0:T(8,128)(2,1)S(1)} %convolution_convert_fusion), channel_id=1, source_target_pairs={{0,16},{8,24},{16,0},{24,8},{32,48},{40,56},{48,32},{56,40},{64,80... | collective-permute-start | bytes 6291464 | tf_op jit(solution)/shard_map/ppermute | solution.py:15
Sparse Core Ops, SparseCore 0:
  154.6 32.6 reduce-scatter.1
where the time goes:
time: 271 us; the launch traced here: 267 us
  waiting for transfers between devices  169 us (62%)
  matrix products  45.1 us (17%)
  blocking collectives  23 us (8%)
  between operations  14.2 us (5%)
  other arithmetic  8.62 us (3%)
  starting transfers between devices  5.92 us (2%)
    ppermute x4, waiting for transfers between devices, partner(): return lax.ppermute(value, axis, pairs)  169 us
    psum x1, blocking collectives, on_device(): lax.psum((local_sum * jnp.exp(local_maximum - row_maximum), positive_part...  13 us
    dot_general x2, matrix products, on_device(): jnp.einsum('qd,pd->qp', queries, block_rows, preferred_element_type=jnp.f...  11.9 us
    dot_general x2, matrix products, on_device(): jnp.dot(weights_round, block_rows, preferred_element_type=jnp.float32)  11.2 us
    pmax x1, blocking collectives, on_device(): row_maximum = lax.pmax(local_maximum, 'pcol')  10 us
    dot_general x2, matrix products, on_device(): jnp.einsum('qp,qd->pd', round_weights[round_index], queries, preferred_el...  8.52 us
    ppermute x4, starting transfers between devices, partner(): return lax.ppermute(value, axis, pairs)  5.88 us
    dot_general x1, matrix products, on_device(): jnp.dot(own_weights, passages, preferred_element_type=jnp.float32)  5.57 us
  transfers between devices with their start and end apart: 5, of which 4 were waited for; matrix products, arithmetic and copies ran while one was open for 9% of the time, Pallas kernels for 0%

commit v1 on v0

v1 whole, which is shorter than its diff:
```python
import functools

import jax
import jax.numpy as jnp
from jax import lax
from jax.experimental import pallas as pl
from jax.experimental.pallas import tpu as pltpu
from jax.sharding import PartitionSpec as P

F32 = jnp.float32
BF16 = jnp.bfloat16
D = 1024
SHARD = 1024
CHIP = 2048
UNIT = 128
BATCH = 256
QUERIES = 512
NB = 2
LOW = -1e30
MESH = pl.DeviceIdType.MESH


def dot_nt(a, b):
    return lax.dot_general(a, b, (((1,), (1,)), ((), ())), preferred_element_type=F32)


def dot_nn(a, b):
    return jnp.dot(a, b, preferred_element_type=F32)


def kernel(
    q_hbm, p_hbm, mask_ref, pos_ref,
    loss_ref, qg_ref, pg_hbm,
    qv, pv, pt, lg, ev, tf, t0,
    sb, rb, sa, ra, sy, ry, acc,
    pgs, pgr, pgo, pgv,
    st, sty, stc, stx, sc, ls, lr,
    load_sem, out_sem, pair_send, pair_recv,
    qa_send, qa_recv, qb_send, qb_recv, qy_send, qy_recv,
    sty_send, sty_recv, stx_send, stx_recv,
    tb_send, tb_recv, ta_send, ta_recv, ty_send, ty_recv,
):
    g = lax.axis_index("qgrp")
    k = lax.axis_index("pcol")
    x = lax.rem(g, 4)
    y = lax.div(k, 2)
    c = lax.rem(k, 2)
    h = lax.rem(y, 2)
    g1 = g + 1 - 2 * lax.rem(x, 2)
    g2 = g + 2 - 4 * lax.div(x, 2)
    g3 = g + 3 - 2 * x
    up = (g, lax.rem(k + 2, 8))
    far = (g, lax.rem(k + 4, 8))
    down = (g, lax.rem(k + 6, 8))
    pair = (g, k + 1 - 2 * c)
    n1, n2, n3 = (g1, k), (g2, k), (g3, k)

    def rcopy(src, dst, ssem, rsem, dev):
        return pltpu.make_async_remote_copy(
            src_ref=src, dst_ref=dst, send_sem=ssem, recv_sem=rsem,
            device_id=dev, device_id_type=MESH,
        )

    q_load = pltpu.make_async_copy(q_hbm.at[:, c], qv.at[0], load_sem.at[0])
    p_load = pltpu.make_async_copy(p_hbm, pv.at[0], load_sem.at[1])
    q_load.start()
    p_load.start()

    barrier = pltpu.get_barrier_semaphore()
    for dev in (up, far, down, pair, n1, n2, n3):
        pl.semaphore_signal(barrier, inc=1, device_id=dev, device_id_type=MESH)
    pl.semaphore_wait(barrier, 7)

    p_swap = rcopy(p_hbm, pv.at[1], pair_send.at[0], pair_recv.at[0], pair)
    sends = [p_swap]

    def start(copy):
        copy.start()
        sends.append(copy)

    def rows(s):
        return pl.ds(64 * s, 64)

    def qa(b, s):
        return rcopy(
            q_hbm.at[2 * b + h, c, rows(s)], qv.at[1, 2 * b + h, rows(s)],
            qa_send.at[b, s], qa_recv.at[b, s], n1,
        )

    def qb(b, s):
        return rcopy(
            qv.at[1, 2 * b + h, rows(s)], qv.at[2, 2 * b + h, rows(s)],
            qb_send.at[b, s], qb_recv.at[b, s], n3,
        )

    def qy(b, r, s):
        return rcopy(
            qv.at[1 + r, 2 * b + h, rows(s)], qv.at[1 + r, 2 * b + h, rows(s)],
            qy_send.at[b, r, s], qy_recv.at[b, r, s], (up, down)[s],
        )

    def qy_wait(b, r):
        for s in range(2):
            block = qv.at[1 + r, 2 * b + 1 - h, rows(s)]
            rcopy(
                block, block, qy_send.at[b, r, s], qy_recv.at[b, r, s], (up, down)[s]
            ).wait_recv()

    for b in range(NB):
        for s in range(2):
            start(qa(b, s))
    p_swap.start()

    def forward_a(b):
        for s in range(2):
            qa(b, s).wait_recv()
            start(qb(b, s))
            start(qy(b, 0, s))

    def forward_b(b):
        for s in range(2):
            qb(b, s).wait_recv()
            start(qy(b, 1, s))

    flags = [mask_ref[0, g1] > 0, mask_ref[1, g2] > 0]

    def positive_row(b):
        return jnp.concatenate(
            [pos_ref[pl.ds(2 * (2 * b + j) + c, 1), :] for j in range(2)], axis=1
        )

    def first_column(half):
        return (k if half == 0 else k + 1 - 2 * c) * SHARD

    ls[...] = jnp.zeros((8, UNIT), F32)
    q_load.wait()
    p_load.wait()
    own_max = jnp.full((1, QUERIES), LOW, F32)

    def own_logits(half, peak):
        def body(i, peak):
            own_queries = qv[0].reshape(QUERIES, D)
            block = dot_nt(pv[half, pl.ds(i * 512, 512), :], own_queries)
            lg[pl.ds(half * SHARD + i * 512, 512), :] = block
            return jnp.maximum(peak, jnp.max(block, axis=0, keepdims=True))

        return lax.fori_loop(0, 2, body, peak)

    own_max = own_logits(0, own_max)
    forward_a(0)
    p_swap.wait_recv()
    own_max = own_logits(1, own_max)
    forward_b(0)

    positive_all = jnp.concatenate([positive_row(b) for b in range(NB)], axis=1)

    def own_exp(half, carry):
        def body(i, carry):
            total, positive = carry
            r = half * SHARD + i * 256
            block = lg[pl.ds(r, 256), :]
            column = lax.broadcasted_iota(jnp.int32, (256, QUERIES), 0) + (
                first_column(half) + i * 256
            )
            e = jnp.exp(block - own_max)
            ev[0, pl.ds(r, 256), :] = e.astype(BF16)
            total = total + jnp.sum(e, axis=0, keepdims=True)
            positive = positive + jnp.sum(
                jnp.where(column == positive_all, block, 0.0), axis=0, keepdims=True
            )
            return total, positive

        return lax.fori_loop(0, 4, body, carry)

    zero = jnp.zeros((1, QUERIES), F32)
    own_total, own_positive = own_exp(1, own_exp(0, (zero, zero)))
    for b in range(NB):
        part = slice(b * BATCH, (b + 1) * BATCH)
        st[b, 0:1, :] = own_max[:, part]
        st[b, 3:4, :] = own_total[:, part]
        st[b, 6:7, :] = own_positive[:, part]
        st[b, 7:8, :] = jnp.zeros((1, BATCH), F32)

    for half in range(2):
        @pl.loop(0, 4)
        def _(i):
            pt[half * 4 + i] = pv[half, pl.ds(i * 256, 256), :].T

    forward_a(1)

    def lent(b, r):
        def body(i, peak):
            queries = qv[1 + r, 2 * b:2 * b + 2].reshape(BATCH, D)
            half, rest = lax.div(i, 2), lax.rem(i, 2)
            block = dot_nt(pv[half, pl.ds(rest * 512, 512), :], queries)
            lg[pl.ds(i * 512, 512), 0:BATCH] = block
            return jnp.maximum(peak, jnp.max(block, axis=0, keepdims=True))

        peak = lax.fori_loop(0, 4, body, jnp.full((1, BATCH), LOW, F32))

        def exp_body(i, total):
            e = jnp.exp(lg[pl.ds(i * 256, 256), 0:BATCH] - peak)
            ev[1 + r, pl.ds(i * 256, 256), b * BATCH:(b + 1) * BATCH] = e.astype(BF16)
            return total + jnp.sum(e, axis=0, keepdims=True)

        total = lax.fori_loop(0, 8, exp_body, jnp.zeros((1, BATCH), F32))
        st[b, 1 + r:2 + r, :] = jnp.where(flags[r], peak, LOW)
        st[b, 4 + r:5 + r, :] = total

    def stats_y(b, i):
        dev = (down, far, up)[i]
        return rcopy(st.at[b], sty.at[b, i], sty_send.at[b, i], sty_recv.at[b, i], dev)

    def stats_x(b, i):
        dev = (n1, n2, n3)[i]
        return rcopy(stc.at[b], stx.at[b, i], stx_send.at[b, i], stx_recv.at[b, i], dev)

    def combine_y(b):
        for i in range(3):
            stats_y(b, i).wait_recv()
        peaks = [st[b, 0:3, :]] + [sty[b, i, 0:3, :] for i in range(3)]
        sums = [st[b, 3:6, :]] + [sty[b, i, 3:6, :] for i in range(3)]
        peak = functools.reduce(jnp.maximum, peaks)
        total = sum(s * jnp.exp(m - peak) for s, m in zip(sums, peaks))
        positive = st[b, 6:7, :] + sty[b, 0, 6:7, :] + sty[b, 1, 6:7, :] + sty[b, 2, 6:7, :]
        stc[b, 0:3, :] = peak
        stc[b, 3:6, :] = total
        stc[b, 6:7, :] = positive
        stc[b, 7:8, :] = jnp.zeros((1, BATCH), F32)

    def combine_x(b):
        for i in range(3):
            stats_x(b, i).wait_recv()
        own, one, two, three = stc[b], stx[b, 0], stx[b, 1], stx[b, 2]
        sources = (
            ((own, 0), (one, 1), (two, 2)),
            ((one, 0), (own, 1), (three, 2)),
            ((two, 0), (own, 2), (three, 1)),
        )
        log_totals = []
        for source in sources:
            peaks = [a[r:r + 1] for a, r in source]
            sums = [a[3 + r:4 + r] for a, r in source]
            peak = functools.reduce(jnp.maximum, peaks)
            total = sum(s * jnp.exp(m - peak) for s, m in zip(sums, peaks))
            log_totals.append(peak + jnp.log(total))
        for r in range(3):
            sc[b, r:r + 1, :] = jnp.exp(st[b, r:r + 1, :] - log_totals[r])
        positive = own[6:7]
        sc[b, 3:4, :] = jnp.exp(positive - log_totals[0]) - 1.0
        loss = log_totals[0] - positive
        for j in range(2):
            ls[2 * b + j:2 * b + j + 1, :] = loss[:, j * UNIT:(j + 1) * UNIT]

    def terms(b, r):
        @pl.loop(0, 4)
        def _(i):
            total = None
            for n in range(8):
                part = dot_nn(
                    pt[n, pl.ds(i * 256, 256), :],
                    ev[r, n * 256:(n + 1) * 256, b * BATCH:(b + 1) * BATCH],
                )
                total = part if total is None else total + part
            if r == 0:
                t0[b, pl.ds(i * 256, 256), :] = total
            else:
                tf[b, r - 1, pl.ds(i * 256, 256), :] = total

    def own_weights(b):
        scale, less = sc[b, 0:1, :], sc[b, 3:4, :]
        where = positive_row(b)
        for half in range(2):
            @pl.loop(0, 4)
            def _(i):
                span = pl.ds(half * SHARD + i * 256, 256)
                column = lax.broadcasted_iota(jnp.int32, (256, BATCH), 0) + (
                    first_column(half) + i * 256
                )
                e = ev[0, span, b * BATCH:(b + 1) * BATCH].astype(F32)
                w = jnp.where(column == where, less, e * scale)
                ev[0, span, b * BATCH:(b + 1) * BATCH] = w.astype(BF16)

    def lent_weights(b, r):
        scale = sc[b, 1 + r:2 + r, :]

        @pl.loop(0, 8)
        def _(i):
            span = pl.ds(i * 256, 256)
            e = ev[1 + r, span, b * BATCH:(b + 1) * BATCH].astype(F32)
            ev[1 + r, span, b * BATCH:(b + 1) * BATCH] = (e * scale).astype(BF16)

    def tb(b, j):
        return rcopy(sb.at[b, j], rb.at[b, j], tb_send.at[b, j], tb_recv.at[b, j], n3)

    def ta(b, j):
        return rcopy(sa.at[b, j], ra.at[b, j], ta_send.at[b, j], ta_recv.at[b, j], n1)

    def ty(b, j):
        unit = 2 * b + j
        slot = lax.rem(y - unit + 4, 4) - 1
        return rcopy(
            sy.at[b, j], ry.at[slot], ty_send.at[b, j], ty_recv.at[slot], (g, 2 * unit + c)
        )

    def lanes(j):
        return slice(j * UNIT, (j + 1) * UNIT)

    def send_b(b):
        for j in range(2):
            sb[b, j] = (tf[b, 1, :, lanes(j)] * sc[b, 2:3, lanes(j)]).astype(BF16)
            start(tb(b, j))

    def send_a(b):
        for j in range(2):
            tb(b, j).wait_recv()
            sa[b, j] = (
                tf[b, 0, :, lanes(j)] * sc[b, 1:2, lanes(j)] + rb[b, j].astype(F32)
            ).astype(BF16)
            start(ta(b, j))

    def send_y(b):
        for j in range(2):
            unit = 2 * b + j
            ta(b, j).wait_recv()

            @pl.when(y == unit)
            def _():
                acc[...] = t0[b, :, lanes(j)] + ra[b, j].astype(F32)

            @pl.when(y != unit)
            def _():
                sy[b, j] = (t0[b, :, lanes(j)] + ra[b, j].astype(F32)).astype(BF16)
                ty(b, j).start()

    def passage_part(half, target):
        @pl.loop(0, 4)
        def _(i):
            total = None
            for r in range(3):
                part = dot_nn(
                    ev[r, pl.ds(half * SHARD + i * 256, 256), :], qv[r].reshape(QUERIES, D)
                )
                total = part if total is None else total + part
            target[pl.ds(i * 256, 256), :] = total.astype(target.dtype)

    qy_wait(0, 0)
    lent(0, 0)
    forward_b(1)
    qy_wait(0, 1)
    lent(0, 1)
    for i in range(3):
        start(stats_y(0, i))
    terms(0, 2)
    combine_y(0)
    for i in range(3):
        start(stats_x(0, i))
    terms(0, 1)
    combine_x(0)
    send_b(0)
    qy_wait(1, 0)
    lent(1, 0)
    qy_wait(1, 1)
    lent(1, 1)
    for i in range(3):
        start(stats_y(1, i))
    terms(1, 2)
    combine_y(1)
    for i in range(3):
        start(stats_x(1, i))
    terms(1, 1)
    combine_x(1)
    send_b(1)
    loss_copy = rcopy(ls, lr, pair_send.at[1], pair_recv.at[1], pair)
    start(loss_copy)
    send_a(0)
    own_weights(0)
    terms(0, 0)
    own_weights(1)
    terms(1, 0)
    for b in range(NB):
        for r in range(2):
            lent_weights(b, r)
    send_a(1)
    send_y(0)
    passage_part(1, pgs)
    pg_copy = rcopy(pgs, pgr, pair_send.at[2], pair_recv.at[2], pair)
    start(pg_copy)
    passage_part(0, pgo)
    send_y(1)
    loss_copy.wait_recv()
    for j in range(4):
        loss_ref[pl.ds(2 * j + c, 1), :] = ls[j:j + 1, :]
        loss_ref[pl.ds(2 * j + 1 - c, 1), :] = lr[j:j + 1, :]
    pg_copy.wait_recv()
    outs = []
    for i in range(4):
        span = pl.ds(i * 256, 256)
        pgv[span, :] = (pgo[span, :] + pgr[span, :].astype(F32)).astype(BF16)
        out = pltpu.make_async_copy(pgv.at[span], pg_hbm.at[span], out_sem.at[i])
        out.start()
        outs.append(out)
    total = acc[...]
    for slot in range(3):
        rcopy(sy.at[0, 0], ry.at[slot], ty_send.at[0, 0], ty_recv.at[slot], up).wait_recv()
        total = total + ry[slot].astype(F32)
    qg_ref[...] = total.T.astype(BF16)
    for copy in sends:
        copy.wait_send()
    for b in range(NB):
        for j in range(2):
            @pl.when(y != 2 * b + j)
            def _():
                ty(b, j).wait_send()
    for out in outs:
        out.wait()


def on_device(queries, passages, block_mask, positives):
    vmem = pltpu.VMEM
    dma = pltpu.SemaphoreType.DMA
    loss, query_grad, passage_grad = pl.pallas_call(
        kernel,
        out_shape=(
            jax.ShapeDtypeStruct((8, 128), F32),
            jax.ShapeDtypeStruct((UNIT, D), BF16),
            jax.ShapeDtypeStruct((SHARD, D), BF16),
        ),
        in_specs=[
            pl.BlockSpec(memory_space=pl.ANY),
            pl.BlockSpec(memory_space=pl.ANY),
            pl.BlockSpec(memory_space=pltpu.SMEM),
            pl.BlockSpec(memory_space=pltpu.VMEM),
        ],
        out_specs=(
            pl.BlockSpec(memory_space=pltpu.VMEM),
            pl.BlockSpec(memory_space=pltpu.VMEM),
            pl.BlockSpec(memory_space=pl.ANY),
        ),
        scratch_shapes=[
            vmem((3, 4, UNIT, D), BF16),
            vmem((2, SHARD, D), BF16),
            vmem((8, D, 256), BF16),
            vmem((CHIP, QUERIES), F32),
            vmem((3, CHIP, QUERIES), BF16),
            vmem((NB, 2, D, BATCH), F32),
            vmem((NB, D, BATCH), F32),
            vmem((NB, 2, D, UNIT), BF16),
            vmem((NB, 2, D, UNIT), BF16),
            vmem((NB, 2, D, UNIT), BF16),
            vmem((NB, 2, D, UNIT), BF16),
            vmem((NB, 2, D, UNIT), BF16),
            vmem((3, D, UNIT), BF16),
            vmem((D, UNIT), F32),
            vmem((SHARD, D), BF16),
            vmem((SHARD, D), BF16),
            vmem((SHARD, D), F32),
            vmem((SHARD, D), BF16),
            vmem((NB, 8, BATCH), F32),
            vmem((NB, 3, 8, BATCH), F32),
            vmem((NB, 8, BATCH), F32),
            vmem((NB, 3, 8, BATCH), F32),
            vmem((NB, 8, BATCH), F32),
            vmem((8, UNIT), F32),
            vmem((8, UNIT), F32),
            dma((2,)), dma((4,)), dma((3,)), dma((3,)),
            dma((NB, 2)), dma((NB, 2)), dma((NB, 2)), dma((NB, 2)),
            dma((NB, 2, 2)), dma((NB, 2, 2)),
            dma((NB, 3)), dma((NB, 3)), dma((NB, 3)), dma((NB, 3)),
            dma((NB, 2)), dma((NB, 2)), dma((NB, 2)), dma((NB, 2)),
            dma((NB, 2)), dma((3,)),
        ],
        compiler_params=pltpu.CompilerParams(
            collective_id=0, has_side_effects=True, vmem_limit_bytes=60 * 1024 * 1024
        ),
        cost_estimate=pl.CostEstimate(
            flops=9 * 2 * 1024**3, bytes_accessed=7 * 2**20, transcendentals=3 * 2**20
        ),
    )(
        queries.reshape(4, 2, UNIT, D),
        passages,
        block_mask,
        positives.reshape(8, UNIT),
    )
    return loss.reshape(1024), query_grad, passage_grad


def solution(mesh):
    in_specs = (P("qgrp", None), P(("qgrp", "pcol"), None), P(), P("qgrp"))
    out_specs = (P("qgrp"), P(("qgrp", "pcol"), None), P(("qgrp", "pcol"), None))
    return jax.shard_map(
        on_device, mesh=mesh, in_specs=in_specs, out_specs=out_specs, check_vma=False
    )
```

time: 271 us -> 85.6 us (0.32); the launches traced: 267 us -> 85.3 us
  waiting for transfers between devices: 169 us -> 0 us
  Pallas kernels: 0 us -> 78.7 us
  matrix products: 45.1 us -> 0 us
  blocking collectives: 23 us -> 0 us
  between operations: 14.2 us -> 0.64 us
  other arithmetic: 8.62 us -> 0 us
  starting transfers between devices: 5.92 us -> 0 us
  local copies, waits for them, and re-layouts: 1.28 us -> 6.01 us
    ppermute x4 -> x0, waiting for transfers between devices: 169 us -> none  [partner(): return lax.ppermute(value, axis, pairs)]
    pallas_call x0 -> x1, Pallas kernels: none -> 78.7 us  [on_device(): pl.pallas_call(kernel, out_shape=(jax.ShapeDtypeStruct((8, 128), F32), ja...]
    dot_general x9 -> x0, matrix products: 45.1 us -> none  [the longest x2 11.9 us: on_device(): jnp.einsum('qd,pd->qp', queries, block_rows, preferred_element_type=jnp.f...]
    psum x1 -> x0, blocking collectives: 13 us -> none  [on_device(): lax.psum((local_sum * jnp.exp(local_maximum - row_maximum), positive_part...]
    pmax x1 -> x0, blocking collectives: 10 us -> none  [on_device(): row_maximum = lax.pmax(local_maximum, 'pcol')]
    ppermute x4 -> x0, starting transfers between devices: 5.88 us -> none  [partner(): return lax.ppermute(value, axis, pairs)]
    unnamed x16 -> x3, local copies, waits for them, and re-layouts: 0.52 us -> 6.01 us
    reduce_sum x3 -> x0, other arithmetic: 4.99 us -> none  [the longest x2 3.59 us: block_stats(): return (peak, jnp.sum(jnp.exp(logits - peak[:, None]), axis=1))]
  transfers between devices with their start and end apart: 5 -> 0, of which waited for: 4 -> 0; matrix products, arithmetic and copies ran while one was open for 9% -> 0% of each run, Pallas kernels for 0% -> 0%
where the time goes in v1:
time: 85.6 us; the launch traced here: 85.3 us
  Pallas kernels  78.7 us (92%)
  local copies, waits for them, and re-layouts  6.01 us (7%)
    pallas_call x1, Pallas kernels, on_device(): pl.pallas_call(kernel, out_shape=(jax.ShapeDtypeStruct((8, 128), F32), ja...  78.7 us
    unnamed x3, local copies, waits for them, and re-layouts  6.01 us

profile of v1, /device:TPU:24, one launch (start us, length us, event | category | flops | bytes accessed | tf_op | source)
XLA Modules:
  0.0 85.3 jit_solution(7958671061845160167)
XLA Ops:
  0.6 78.7 %shard_map.67 = (f32[8,128]{1,0:T(8,128)}, bf16[128,1024]{1,0:T(8,128)(2,1)}, bf16[1024,1024]{1,0:T(8,128)(2,1)}) custom-call(bf16[4,2,128,1024]{3,2,1,0:T(8,128)(2,1)} %bitcast.4, bf16[1024,1024]{1,0:T(8,128)(2,1)} %p_hbm.1, s32[2,16]{1,0:T(2,128)} %mask_ref.1, s32[8,128]{1,0:T(8,128)} %bitcast.5), custom_call_target="tpu_custom_call" | custom-call | flops 19327352832 | bytes 7340032 | tf_op jit(solution)/shard_map/pallas_call | solution.py:422
  79.3 1.3 %copy.10 = f32[1024]{0:T(1024)} copy(f32[1024]{0:T(1024)} %bitcast.3) | data formatting | bytes 8192
  80.6 1.7 %copy.11 = bf16[128,1024]{1,0:T(8,128)(2,1)} copy(bf16[128,1024]{1,0:T(8,128)(2,1)} %get-tuple-element.13) | data formatting | bytes 524288
  82.2 3.1 %copy.12 = bf16[1024,1024]{1,0:T(8,128)(2,1)} copy(bf16[1024,1024]{1,0:T(8,128)(2,1)} %get-tuple-element.14) | data formatting | bytes 4194304

commit v2 on v1

--- a/solution.py
+++ b/solution.py
@@ -16,6 +16,8 @@
 BATCH = 256
 QUERIES = 512
 NB = 2
+PIECES = 4
+HALF = 512
 LOW = -1e30
 MESH = pl.DeviceIdType.MESH
 
@@ -31,13 +33,13 @@
 def kernel(
     q_hbm, p_hbm, mask_ref, pos_ref,
     loss_ref, qg_ref, pg_hbm,
-    qv, pv, pt, lg, ev, tf, t0,
+    qv, pv, pt, lg, ev, t1, t0,
     sb, rb, sa, ra, sy, ry, acc,
     pgs, pgr, pgo, pgv,
-    st, sty, stc, stx, sc, ls, lr,
+    st, sty, stm, stc, stx, sc, ls, lr,
     load_sem, out_sem, pair_send, pair_recv,
     qa_send, qa_recv, qb_send, qb_recv, qy_send, qy_recv,
-    sty_send, sty_recv, stx_send, stx_recv,
+    sty_send, sty_recv, stx_send, stx_recv, stm_send, stm_recv,
     tb_send, tb_recv, ta_send, ta_recv, ty_send, ty_recv,
 ):
     g = lax.axis_index("qgrp")
@@ -61,10 +63,15 @@
             device_id=dev, device_id_type=MESH,
         )
 
-    q_load = pltpu.make_async_copy(q_hbm.at[:, c], qv.at[0], load_sem.at[0])
-    p_load = pltpu.make_async_copy(p_hbm, pv.at[0], load_sem.at[1])
-    q_load.start()
-    p_load.start()
+    loads = [pltpu.make_async_copy(p_hbm, pv.at[0], load_sem.at[NB * 2])]
+    for b in range(NB):
+        for j in range(2):
+            slot = 2 * b + j
+            loads.append(
+                pltpu.make_async_copy(q_hbm.at[b + 2 * j, c], qv.at[0, slot], load_sem.at[slot])
+            )
+    for copy in loads:
+        copy.start()
 
     barrier = pltpu.get_barrier_semaphore()
     for dev in (up, far, down, pair, n1, n2, n3):
@@ -78,63 +85,61 @@
         copy.start()
         sends.append(copy)
 
-    def rows(s):
-        return pl.ds(64 * s, 64)
-
-    def qa(b, s):
+    def rows(i):
+        return pl.ds(64 * (i % 2) + 32 * (i // 2), 32)
+
+    def qa(b, i):
         return rcopy(
-            q_hbm.at[2 * b + h, c, rows(s)], qv.at[1, 2 * b + h, rows(s)],
-            qa_send.at[b, s], qa_recv.at[b, s], n1,
-        )
-
-    def qb(b, s):
+            q_hbm.at[b + 2 * h, c, rows(i)], qv.at[1, 2 * b + h, rows(i)],
+            qa_send.at[b, i], qa_recv.at[b, i], n1,
+        )
+
+    def qb(b, i):
         return rcopy(
-            qv.at[1, 2 * b + h, rows(s)], qv.at[2, 2 * b + h, rows(s)],
-            qb_send.at[b, s], qb_recv.at[b, s], n3,
-        )
-
-    def qy(b, r, s):
+            qv.at[1, 2 * b + h, rows(i)], qv.at[2, 2 * b + h, rows(i)],
+            qb_send.at[b, i], qb_recv.at[b, i], n3,
+        )
+
+    def qy(b, r, i):
+        block = qv.at[1 + r, 2 * b + h, rows(i)]
         return rcopy(
-            qv.at[1 + r, 2 * b + h, rows(s)], qv.at[1 + r, 2 * b + h, rows(s)],
-            qy_send.at[b, r, s], qy_recv.at[b, r, s], (up, down)[s],
+            block, block, qy_send.at[b, r, i], qy_recv.at[b, r, i], (up, down)[i % 2]
         )
 
     def qy_wait(b, r):
-        for s in range(2):
-            block = qv.at[1 + r, 2 * b + 1 - h, rows(s)]
+        for i in range(PIECES):
+            block = qv.at[1 + r, 2 * b + 1 - h, rows(i)]
             rcopy(
-                block, block, qy_send.at[b, r, s], qy_recv.at[b, r, s], (up, down)[s]
+                block, block, qy_send.at[b, r, i], qy_recv.at[b, r, i], (up, down)[i % 2]
             ).wait_recv()
 
     for b in range(NB):
-        for s in range(2):
-            start(qa(b, s))
+        for i in range(PIECES):
+            start(qa(b, i))
     p_swap.start()
 
-    def forward_a(b):
-        for s in range(2):
-            qa(b, s).wait_recv()
-            start(qb(b, s))
-            start(qy(b, 0, s))
-
-    def forward_b(b):
-        for s in range(2):
-            qb(b, s).wait_recv()
-            start(qy(b, 1, s))
+    def forward_a(b, i):
+        qa(b, i).wait_recv()
+        start(qb(b, i))
+        start(qy(b, 0, i))
+
+    def forward_b(b, i):
+        qb(b, i).wait_recv()
+        start(qy(b, 1, i))
 
     flags = [mask_ref[0, g1] > 0, mask_ref[1, g2] > 0]
 
     def positive_row(b):
         return jnp.concatenate(
-            [pos_ref[pl.ds(2 * (2 * b + j) + c, 1), :] for j in range(2)], axis=1
+            [pos_ref[pl.ds(2 * (b + 2 * j) + c, 1), :] for j in range(2)], axis=1
         )
 
     def first_column(half):
         return (k if half == 0 else k + 1 - 2 * c) * SHARD
 
     ls[...] = jnp.zeros((8, UNIT), F32)
-    q_load.wait()
-    p_load.wait()
+    for copy in loads:
+        copy.wait()
     own_max = jnp.full((1, QUERIES), LOW, F32)
 
     def own_logits(half, peak):
@@ -146,11 +151,24 @@
 
         return lax.fori_loop(0, 2, body, peak)
 
+    def transpose(half):
+        for i in range(4):
+            first = half * SHARD + i * 256
+            pt[:, first:first + 256] = pv[half, pl.ds(i * 256, 256), :].T
+
     own_max = own_logits(0, own_max)
-    forward_a(0)
+    transpose(0)
+    forward_a(0, 0)
+    forward_a(0, 1)
     p_swap.wait_recv()
     own_max = own_logits(1, own_max)
-    forward_b(0)
+    forward_a(0, 2)
+    forward_b(0, 0)
+    forward_a(0, 3)
+    forward_b(0, 1)
+    transpose(1)
+    forward_a(1, 0)
+    forward_b(0, 2)
 
     positive_all = jnp.concatenate([positive_row(b) for b in range(NB)], axis=1)
 
@@ -173,7 +191,10 @@
         return lax.fori_loop(0, 4, body, carry)
 
     zero = jnp.zeros((1, QUERIES), F32)
-    own_total, own_positive = own_exp(1, own_exp(0, (zero, zero)))
+    own_sums = own_exp(0, (zero, zero))
+    forward_a(1, 1)
+    forward_b(0, 3)
+    own_total, own_positive = own_exp(1, own_sums)
     for b in range(NB):
         part = slice(b * BATCH, (b + 1) * BATCH)
         st[b, 0:1, :] = own_max[:, part]
@@ -181,22 +202,14 @@
         st[b, 6:7, :] = own_positive[:, part]
         st[b, 7:8, :] = jnp.zeros((1, BATCH), F32)
 
-    for half in range(2):
-        @pl.loop(0, 4)
-        def _(i):
-            pt[half * 4 + i] = pv[half, pl.ds(i * 256, 256), :].T
-
-    forward_a(1)
-
     def lent(b, r):
-        def body(i, peak):
+        def body(half, peak):
             queries = qv[1 + r, 2 * b:2 * b + 2].reshape(BATCH, D)
-            half, rest = lax.div(i, 2), lax.rem(i, 2)
-            block = dot_nt(pv[half, pl.ds(rest * 512, 512), :], queries)
-            lg[pl.ds(i * 512, 512), 0:BATCH] = block
+            block = dot_nt(pv[half], queries)
+            lg[pl.ds(half * SHARD, SHARD), 0:BATCH] = block
             return jnp.maximum(peak, jnp.max(block, axis=0, keepdims=True))
 
-        peak = lax.fori_loop(0, 4, body, jnp.full((1, BATCH), LOW, F32))
+        peak = lax.fori_loop(0, 2, body, jnp.full((1, BATCH), LOW, F32))
 
         def exp_body(i, total):
             e = jnp.exp(lg[pl.ds(i * 256, 256), 0:BATCH] - peak)
@@ -210,6 +223,9 @@
     def stats_y(b, i):
         dev = (down, far, up)[i]
         return rcopy(st.at[b], sty.at[b, i], sty_send.at[b, i], sty_recv.at[b, i], dev)
+
+    def stats_m(b):
+        return rcopy(st.at[b], stm.at[b], stm_send.at[b], stm_recv.at[b], n3)
 
     def stats_x(b, i):
         dev = (n1, n2, n3)[i]
@@ -246,26 +262,23 @@
             log_totals.append(peak + jnp.log(total))
         for r in range(3):
             sc[b, r:r + 1, :] = jnp.exp(st[b, r:r + 1, :] - log_totals[r])
+        stats_m(b).wait_recv()
+        sc[b, 4:5, :] = jnp.exp(stm[b, 2:3, :] - log_totals[1])
         positive = own[6:7]
         sc[b, 3:4, :] = jnp.exp(positive - log_totals[0]) - 1.0
         loss = log_totals[0] - positive
         for j in range(2):
-            ls[2 * b + j:2 * b + j + 1, :] = loss[:, j * UNIT:(j + 1) * UNIT]
+            ls[b + 2 * j:b + 2 * j + 1, :] = loss[:, j * UNIT:(j + 1) * UNIT]
+
+    def term(b, r, i):
+        return dot_nn(pt[pl.ds(i * HALF, HALF), :], ev[r, :, b * BATCH:(b + 1) * BATCH])
 
     def terms(b, r):
-        @pl.loop(0, 4)
+        target = t0 if r == 0 else t1
+
+        @pl.loop(0, 2)
         def _(i):
-            total = None
-            for n in range(8):
-                part = dot_nn(
-                    pt[n, pl.ds(i * 256, 256), :],
-                    ev[r, n * 256:(n + 1) * 256, b * BATCH:(b + 1) * BATCH],
-                )
-                total = part if total is None else total + part
-            if r == 0:
-                t0[b, pl.ds(i * 256, 256), :] = total
-            else:
-                tf[b, r - 1, pl.ds(i * 256, 256), :] = total
+            target[b, pl.ds(i * HALF, HALF), :] = term(b, r, i)
 
     def own_weights(b):
         scale, less = sc[b, 0:1, :], sc[b, 3:4, :]
@@ -290,104 +303,139 @@
             e = ev[1 + r, span, b * BATCH:(b + 1) * BATCH].astype(F32)
             ev[1 + r, span, b * BATCH:(b + 1) * BATCH] = (e * scale).astype(BF16)
 
-    def tb(b, j):
-        return rcopy(sb.at[b, j], rb.at[b, j], tb_send.at[b, j], tb_recv.at[b, j], n3)
-
-    def ta(b, j):
-        return rcopy(sa.at[b, j], ra.at[b, j], ta_send.at[b, j], ta_recv.at[b, j], n1)
-
-    def ty(b, j):
-        unit = 2 * b + j
+    def part(n):
+        return n % 2, pl.ds(HALF * (n // 2), HALF)
+
+    def tb(b, n):
+        j, d = part(n)
+        return rcopy(
+            sb.at[b, j, d], rb.at[b, j, d], tb_send.at[b, n], tb_recv.at[b, n], n3
+        )
+
+    def ta(b, n):
+        j, d = part(n)
+        return rcopy(
+            sa.at[b, j, d], ra.at[b, j, d], ta_send.at[b, n], ta_recv.at[b, n], n1
+        )
+
+    def ty(b, n):
+        j, d = part(n)
+        unit = b + 2 * j
         slot = lax.rem(y - unit + 4, 4) - 1
         return rcopy(
-            sy.at[b, j], ry.at[slot], ty_send.at[b, j], ty_recv.at[slot], (g, 2 * unit + c)
+            sy.at[b, j, d], ry.at[slot, d], ty_send.at[b, n], ty_recv.at[slot, n // 2],
+            (g, 2 * unit + c),
         )
 
     def lanes(j):
         return slice(j * UNIT, (j + 1) * UNIT)
 
-    def send_b(b):
+    def send_b(b, i):
+        total = term(b, 2, i).astype(BF16)
         for j in range(2):
-            sb[b, j] = (tf[b, 1, :, lanes(j)] * sc[b, 2:3, lanes(j)]).astype(BF16)
-            start(tb(b, j))
-
-    def send_a(b):
-        for j in range(2):
-            tb(b, j).wait_recv()
-            sa[b, j] = (
-                tf[b, 0, :, lanes(j)] * sc[b, 1:2, lanes(j)] + rb[b, j].astype(F32)
-            ).astype(BF16)
-            start(ta(b, j))
-
-    def send_y(b):
-        for j in range(2):
-            unit = 2 * b + j
-            ta(b, j).wait_recv()
-
-            @pl.when(y == unit)
-            def _():
-                acc[...] = t0[b, :, lanes(j)] + ra[b, j].astype(F32)
-
-            @pl.when(y != unit)
-            def _():
-                sy[b, j] = (t0[b, :, lanes(j)] + ra[b, j].astype(F32)).astype(BF16)
-                ty(b, j).start()
-
-    def passage_part(half, target):
-        @pl.loop(0, 4)
-        def _(i):
-            total = None
-            for r in range(3):
-                part = dot_nn(
-                    ev[r, pl.ds(half * SHARD + i * 256, 256), :], qv[r].reshape(QUERIES, D)
-                )
-                total = part if total is None else total + part
-            target[pl.ds(i * 256, 256), :] = total.astype(target.dtype)
+            sb[b, j, pl.ds(i * HALF, HALF), :] = total[:, lanes(j)]
+            start(tb(b, 2 * i + j))
+
+    def send_a(b, n):
+        j, d = part(n)
+        tb(b, n).wait_recv()
+        sa[b, j, d] = (
+            t1[b, d, lanes(j)] * sc[b, 1:2, lanes(j)]
+            + rb[b, j, d].astype(F32) * sc[b, 4:5, lanes(j)]
+        ).astype(BF16)
+        start(ta(b, n))
+
+    def send_y(b, n):
+        j, d = part(n)
+        unit = b + 2 * j
+        ta(b, n).wait_recv()
+
+        @pl.when(y == unit)
+        def _():
+            acc[d] = t0[b, d, lanes(j)] + ra[b, j, d].astype(F32)
+
+        @pl.when(y != unit)
+        def _():
+            sy[b, j, d] = (t0[b, d, lanes(j)] + ra[b, j, d].astype(F32)).astype(BF16)
+            ty(b, n).start()
+
+    def passage_part(half, i, target):
+        total = None
+        for r in range(3):
+            add = dot_nn(
+                ev[r, pl.ds(half * SHARD + i * 512, 512), :], qv[r].reshape(QUERIES, D)
+            )
+            total = add if total is None else total + add
+        target[pl.ds(i * 512, 512), :] = total.astype(target.dtype)
+
+    def begin_stats(b):
+        start(stats_m(b))
+        for i in range(3):
+            start(stats_y(b, i))
+
+    def begin_stats_x(b):
+        combine_y(b)
+        for i in range(3):
+            start(stats_x(b, i))
 
     qy_wait(0, 0)
     lent(0, 0)
-    forward_b(1)
+    forward_a(1, 2)
+    forward_b(1, 0)
+    forward_a(1, 3)
+    forward_b(1, 1)
     qy_wait(0, 1)
     lent(0, 1)
-    for i in range(3):
-        start(stats_y(0, i))
-    terms(0, 2)
-    combine_y(0)
-    for i in range(3):
-        start(stats_x(0, i))
+    begin_stats(0)
+    send_b(0, 0)
+    forward_b(1, 2)
+    send_b(0, 1)
+    forward_b(1, 3)
+    begin_stats_x(0)
     terms(0, 1)
-    combine_x(0)
-    send_b(0)
     qy_wait(1, 0)
     lent(1, 0)
+    combine_x(0)
+    send_a(0, 0)
     qy_wait(1, 1)
     lent(1, 1)
-    for i in range(3):
-        start(stats_y(1, i))
-    terms(1, 2)
-    combine_y(1)
-    for i in range(3):
-        start(stats_x(1, i))
+    begin_stats(1)
+    send_a(0, 1)
+    send_b(1, 0)
+    send_b(1, 1)
+    send_a(0, 2)
+    own_weights(0)
+    terms(0, 0)
+    send_a(0, 3)
+    begin_stats_x(1)
+    send_y(0, 0)
+    send_y(0, 1)
     terms(1, 1)
+    lent_weights(0, 0)
+    lent_weights(0, 1)
     combine_x(1)
-    send_b(1)
     loss_copy = rcopy(ls, lr, pair_send.at[1], pair_recv.at[1], pair)
     start(loss_copy)
-    send_a(0)
-    own_weights(0)
-    terms(0, 0)
+    send_y(0, 2)
+    send_a(1, 0)
     own_weights(1)
     terms(1, 0)
-    for b in range(NB):
-        for r in range(2):
-            lent_weights(b, r)
-    send_a(1)
-    send_y(0)
-    passage_part(1, pgs)
+    send_a(1, 1)
+    send_y(0, 3)
+    lent_weights(1, 0)
+    lent_weights(1, 1)
+    passage_part(1, 0, pgs)
+    send_a(1, 2)
+    passage_part(1, 1, pgs)
     pg_copy = rcopy(pgs, pgr, pair_send.at[2], pair_recv.at[2], pair)
     start(pg_copy)
-    passage_part(0, pgo)
-    send_y(1)
+    send_a(1, 3)
+    send_y(1, 0)
+    passage_part(0, 0, pgo)
+    send_y(1, 1)
+    passage_part(0, 1, pgo)
+    send_y(1, 2)
+    send_y(1, 3)
     loss_copy.wait_recv()
     for j in range(4):
         loss_ref[pl.ds(2 * j + c, 1), :] = ls[j:j + 1, :]
@@ -400,20 +448,38 @@
         out = pltpu.make_async_copy(pgv.at[span], pg_hbm.at[span], out_sem.at[i])
         out.start()
         outs.append(out)
-    total = acc[...]
-    for slot in range(3):
-        rcopy(sy.at[0, 0], ry.at[slot], ty_send.at[0, 0], ty_recv.at[slot], up).wait_recv()
-        total = total + ry[slot].astype(F32)
-    qg_ref[...] = total.T.astype(BF16)
+    for i in range(2):
+        d = slice(i * HALF, (i + 1) * HALF)
+        total = acc[d]
+        for slot in range(3):
+            rcopy(
+                sy.at[0, 0, d], ry.at[slot, d], ty_send.at[0, 0], ty_recv.at[slot, i], up
+            ).wait_recv()
+            total = total + ry[slot, d].astype(F32)
+        qg_ref[:, d] = total.T.astype(BF16)
     for copy in sends:
         copy.wait_send()
     for b in range(NB):
-        for j in range(2):
-            @pl.when(y != 2 * b + j)
+        for n in range(4):
+            @pl.when(y != b + 2 * (n % 2))
             def _():
-                ty(b, j).wait_send()
+                ty(b, n).wait_send()
     for out in outs:
         out.wait()
+
+
+def finish(loss_in, qg_in, pg_in, loss_out, qg_out, pg_out, sems):
+    copies = [
+        pltpu.make_async_copy(loss_in, loss_out, sems.at[4]),
+        pltpu.make_async_copy(qg_in, qg_out, sems.at[5]),
+    ]
+    for i in range(4):
+        span = pl.ds(i * 256, 256)
+        copies.append(pltpu.make_async_copy(pg_in.at[span], pg_out.at[span], sems.at[i]))
+    for copy in copies:
+        copy.start()
+    for copy in copies:
+        copy.wait()
 
 
 def on_device(queries, passages, block_mask, positives):
@@ -440,10 +506,10 @@
         scratch_shapes=[
             vmem((3, 4, UNIT, D), BF16),
             vmem((2, SHARD, D), BF16),
-            vmem((8, D, 256), BF16),
+            vmem((D, CHIP), BF16),
             vmem((CHIP, QUERIES), F32),
             vmem((3, CHIP, QUERIES), BF16),
-            vmem((NB, 2, D, BATCH), F32),
+            vmem((NB, D, BATCH), F32),
             vmem((NB, D, BATCH), F32),
             vmem((NB, 2, D, UNIT), BF16),
             vmem((NB, 2, D, UNIT), BF16),
@@ -459,16 +525,17 @@
             vmem((NB, 8, BATCH), F32),
             vmem((NB, 3, 8, BATCH), F32),
             vmem((NB, 8, BATCH), F32),
+            vmem((NB, 8, BATCH), F32),
             vmem((NB, 3, 8, BATCH), F32),
             vmem((NB, 8, BATCH), F32),
             vmem((8, UNIT), F32),
             vmem((8, UNIT), F32),
-            dma((2,)), dma((4,)), dma((3,)), dma((3,)),
-            dma((NB, 2)), dma((NB, 2)), dma((NB, 2)), dma((NB, 2)),
-            dma((NB, 2, 2)), dma((NB, 2, 2)),
-            dma((NB, 3)), dma((NB, 3)), dma((NB, 3)), dma((NB, 3)),
-            dma((NB, 2)), dma((NB, 2)), dma((NB, 2)), dma((NB, 2)),
-            dma((NB, 2)), dma((3,)),
+            dma((2 * NB + 1,)), dma((4,)), dma((3,)), dma((3,)),
+            dma((NB, PIECES)), dma((NB, PIECES)), dma((NB, PIECES)), dma((NB, PIECES)),
+            dma((NB, 2, PIECES)), dma((NB, 2, PIECES)),
+            dma((NB, 3)), dma((NB, 3)), dma((NB, 3)), dma((NB, 3)), dma((NB,)), dma((NB,)),
+            dma((NB, 4)), dma((NB, 4)), dma((NB, 4)), dma((NB, 4)),
+            dma((NB, 4)), dma((3, 2)),
         ],
         compiler_params=pltpu.CompilerParams(
             collective_id=0, has_side_effects=True, vmem_limit_bytes=60 * 1024 * 1024
@@ -482,6 +549,17 @@
         block_mask,
         positives.reshape(8, UNIT),
     )
+    loss, query_grad, passage_grad = pl.pallas_call(
+        finish,
+        out_shape=(
+            jax.ShapeDtypeStruct((8, 128), F32),
+            jax.ShapeDtypeStruct((UNIT, D), BF16),
+            jax.ShapeDtypeStruct((SHARD, D), BF16),
+        ),
+        in_specs=[pl.BlockSpec(memory_space=pl.ANY)] * 3,
+        out_specs=(pl.BlockSpec(memory_space=pl.ANY),) * 3,
+        scratch_shapes=[dma((6,))],
+    )(loss, query_grad, passage_grad)
     return loss.reshape(1024), query_grad, passage_grad
 
 

time: 85.6 us -> 145 us (1.69)
  Pallas kernels: 78.7 us -> 144 us
  local copies, waits for them, and re-layouts: 6.01 us -> 0 us
    pallas_call x0 -> x1, Pallas kernels: none -> 72.8 us  [on_device(): pl.pallas_call(finish, out_shape=(jax.ShapeDtypeStruct((8, 128), F32), ja...]
    pallas_call x1, Pallas kernels: 78.7 us -> 71.4 us  [on_device(): pl.pallas_call(kernel, out_shape=(jax.ShapeDtypeStruct((8, 128), F32), ja...]
    unnamed x3 -> x0, local copies, waits for them, and re-layouts: 6.01 us -> none
where the time goes in v2:
time: 145 us
  Pallas kernels  144 us (99%)
    pallas_call x1, Pallas kernels, on_device(): pl.pallas_call(finish, out_shape=(jax.ShapeDtypeStruct((8, 128), F32), ja...  72.8 us
    pallas_call x1, Pallas kernels, on_device(): pl.pallas_call(kernel, out_shape=(jax.ShapeDtypeStruct((8, 128), F32), ja...  71.4 us

profile of v2, /device:TPU:24, one launch (start us, length us, event | category | flops | bytes accessed | tf_op | source)
XLA Modules:
  0.0 145.0 jit_solution(13801637332817762419)
XLA Ops:
  0.6 71.4 %shard_map.67 = (f32[8,128]{1,0:T(8,128)}, bf16[128,1024]{1,0:T(8,128)(2,1)}, bf16[1024,1024]{1,0:T(8,128)(2,1)}) custom-call(bf16[4,2,128,1024]{3,2,1,0:T(8,128)(2,1)} %bitcast.3, bf16[1024,1024]{1,0:T(8,128)(2,1)} %p_hbm.1, s32[2,16]{1,0:T(2,128)} %mask_ref.1, s32[8,128]{1,0:T(8,128)} %bitcast.4), custom_call_target="tpu_custom_call" | custom-call | flops 19327352832 | bytes 7340032 | tf_op jit(solution)/shard_map/pallas_call | solution.py:488
  72.1 72.8 %shard_map.68 = (f32[8,128]{1,0:T(8,128)}, bf16[128,1024]{1,0:T(8,128)(2,1)}, bf16[1024,1024]{1,0:T(8,128)(2,1)}) custom-call(f32[8,128]{1,0:T(8,128)} %get-tuple-element.9.loss_in, bf16[128,1024]{1,0:T(8,128)(2,1)} %get-tuple-element.10.qg_in, bf16[1024,1024]{1,0:T(8,128)(2,1)} %get-tuple-element.11.pg_in), custom_call_target="tpu_custom_call" | custom-call | tf_op jit(solution)/shard_map/pallas_call | solution.py:552

commit v3 on v2

--- a/solution.py
+++ b/solution.py
@@ -32,12 +32,12 @@
 
 def kernel(
     q_hbm, p_hbm, mask_ref, pos_ref,
-    loss_ref, qg_ref, pg_hbm,
+    loss_ref, qg_ref, pg_ref,
     qv, pv, pt, lg, ev, t1, t0,
     sb, rb, sa, ra, sy, ry, acc,
-    pgs, pgr, pgo, pgv,
+    pgs, pgr, pgo,
     st, sty, stm, stc, stx, sc, ls, lr,
-    load_sem, out_sem, pair_send, pair_recv,
+    load_sem, pair_send, pair_recv,
     qa_send, qa_recv, qb_send, qb_recv, qy_send, qy_recv,
     sty_send, sty_recv, stx_send, stx_recv, stm_send, stm_recv,
     tb_send, tb_recv, ta_send, ta_recv, ty_send, ty_recv,
@@ -441,13 +441,9 @@
         loss_ref[pl.ds(2 * j + c, 1), :] = ls[j:j + 1, :]
         loss_ref[pl.ds(2 * j + 1 - c, 1), :] = lr[j:j + 1, :]
     pg_copy.wait_recv()
-    outs = []
     for i in range(4):
         span = pl.ds(i * 256, 256)
-        pgv[span, :] = (pgo[span, :] + pgr[span, :].astype(F32)).astype(BF16)
-        out = pltpu.make_async_copy(pgv.at[span], pg_hbm.at[span], out_sem.at[i])
-        out.start()
-        outs.append(out)
+        pg_ref[span, :] = (pgo[span, :] + pgr[span, :].astype(F32)).astype(BF16)
     for i in range(2):
         d = slice(i * HALF, (i + 1) * HALF)
         total = acc[d]
@@ -464,22 +460,6 @@
             @pl.when(y != b + 2 * (n % 2))
             def _():
                 ty(b, n).wait_send()
-    for out in outs:
-        out.wait()
-
-
-def finish(loss_in, qg_in, pg_in, loss_out, qg_out, pg_out, sems):
-    copies = [
-        pltpu.make_async_copy(loss_in, loss_out, sems.at[4]),
-        pltpu.make_async_copy(qg_in, qg_out, sems.at[5]),
-    ]
-    for i in range(4):
-        span = pl.ds(i * 256, 256)
-        copies.append(pltpu.make_async_copy(pg_in.at[span], pg_out.at[span], sems.at[i]))
-    for copy in copies:
-        copy.start()
-    for copy in copies:
-        copy.wait()
 
 
 def on_device(queries, passages, block_mask, positives):
@@ -488,9 +468,9 @@
     loss, query_grad, passage_grad = pl.pallas_call(
         kernel,
         out_shape=(
-            jax.ShapeDtypeStruct((8, 128), F32),
-            jax.ShapeDtypeStruct((UNIT, D), BF16),
-            jax.ShapeDtypeStruct((SHARD, D), BF16),
+            pltpu.VMEM((8, 128), F32),
+            pltpu.VMEM((UNIT, D), BF16),
+            pltpu.VMEM((SHARD, D), BF16),
         ),
         in_specs=[
             pl.BlockSpec(memory_space=pl.ANY),
@@ -501,7 +481,7 @@
         out_specs=(
             pl.BlockSpec(memory_space=pltpu.VMEM),
             pl.BlockSpec(memory_space=pltpu.VMEM),
-            pl.BlockSpec(memory_space=pl.ANY),
+            pl.BlockSpec(memory_space=pltpu.VMEM),
         ),
         scratch_shapes=[
             vmem((3, 4, UNIT, D), BF16),
@@ -521,7 +501,6 @@
             vmem((SHARD, D), BF16),
             vmem((SHARD, D), BF16),
             vmem((SHARD, D), F32),
-            vmem((SHARD, D), BF16),
             vmem((NB, 8, BATCH), F32),
             vmem((NB, 3, 8, BATCH), F32),
             vmem((NB, 8, BATCH), F32),
@@ -530,7 +509,7 @@
             vmem((NB, 8, BATCH), F32),
             vmem((8, UNIT), F32),
             vmem((8, UNIT), F32),
-            dma((2 * NB + 1,)), dma((4,)), dma((3,)), dma((3,)),
+            dma((2 * NB + 1,)), dma((3,)), dma((3,)),
             dma((NB, PIECES)), dma((NB, PIECES)), dma((NB, PIECES)), dma((NB, PIECES)),
             dma((NB, 2, PIECES)), dma((NB, 2, PIECES)),
             dma((NB, 3)), dma((NB, 3)), dma((NB, 3)), dma((NB, 3)), dma((NB,)), dma((NB,)),
@@ -538,7 +517,7 @@
             dma((NB, 4)), dma((3, 2)),
         ],
         compiler_params=pltpu.CompilerParams(
-            collective_id=0, has_side_effects=True, vmem_limit_bytes=60 * 1024 * 1024
+            collective_id=0, has_side_effects=True, vmem_limit_bytes=52 * 1024 * 1024
         ),
         cost_estimate=pl.CostEstimate(
             flops=9 * 2 * 1024**3, bytes_accessed=7 * 2**20, transcendentals=3 * 2**20
@@ -549,17 +528,6 @@
         block_mask,
         positives.reshape(8, UNIT),
     )
-    loss, query_grad, passage_grad = pl.pallas_call(
-        finish,
-        out_shape=(
-            jax.ShapeDtypeStruct((8, 128), F32),
-            jax.ShapeDtypeStruct((UNIT, D), BF16),
-            jax.ShapeDtypeStruct((SHARD, D), BF16),
-        ),
-        in_specs=[pl.BlockSpec(memory_space=pl.ANY)] * 3,
-        out_specs=(pl.BlockSpec(memory_space=pl.ANY),) * 3,
-        scratch_shapes=[dma((6,))],
-    )(loss, query_grad, passage_grad)
     return loss.reshape(1024), query_grad, passage_grad
 
 

time: 145 us -> 74.3 us (0.51)
  Pallas kernels: 144 us -> 70.6 us
  local copies, waits for them, and re-layouts: 0 us -> 2.62 us
    pallas_call x2 -> x1, Pallas kernels: 144 us -> 70.6 us  [on_device(): pl.pallas_call(kernel, out_shape=(pltpu.VMEM((8, 128), F32), pltpu.VMEM((...]
    unnamed x0 -> x3, local copies, waits for them, and re-layouts: none -> 2.62 us
where the time goes in v3:
time: 74.3 us; the launch traced here: 73.9 us
  Pallas kernels  70.6 us (95%)
  local copies, waits for them, and re-layouts  2.62 us (4%)
    pallas_call x1, Pallas kernels, on_device(): pl.pallas_call(kernel, out_shape=(pltpu.VMEM((8, 128), F32), pltpu.VMEM((...  70.6 us
    unnamed x3, local copies, waits for them, and re-layouts  2.62 us

profile of v3, /device:TPU:24, one launch (start us, length us, event | category | flops | bytes accessed | tf_op | source)
XLA Modules:
  0.0 73.9 jit_solution(15490223412248477357)
XLA Ops:
  0.6 70.6 %shard_map.67 = (f32[8,128]{1,0:T(8,128)S(1)}, bf16[128,1024]{1,0:T(8,128)(2,1)S(1)}, bf16[1024,1024]{1,0:T(8,128)(2,1)S(1)}) custom-call(bf16[4,2,128,1024]{3,2,1,0:T(8,128)(2,1)} %bitcast.4, bf16[1024,1024]{1,0:T(8,128)(2,1)} %p_hbm.1, s32[2,16]{1,0:T(2,128)} %mask_ref.1, s32[8,128]{1,0:T(8,128)} %bitcast.5), custom_call_target="tpu_custom_call" | custom-call | flops 19327352832 | bytes 7340032 | tf_op jit(solution)/shard_map/pallas_call | solution.py:468
  71.3 0.6 copy.10
  71.9 0.7 copy.11
  72.6 1.3 %copy.12 = bf16[1024,1024]{1,0:T(8,128)(2,1)} copy(bf16[1024,1024]{1,0:T(8,128)(2,1)S(1)} %get-tuple-element.11) | data formatting | bytes 4194304

commit v4 on v3

--- a/solution.py
+++ b/solution.py
@@ -18,6 +18,9 @@
 NB = 2
 PIECES = 4
 HALF = 512
+PARTS = 4
+PART = 256
+ROWS = 256
 LOW = -1e30
 MESH = pl.DeviceIdType.MESH
 
@@ -36,10 +39,10 @@
     qv, pv, pt, lg, ev, t1, t0,
     sb, rb, sa, ra, sy, ry, acc,
     pgs, pgr, pgo,
-    st, sty, stm, stc, stx, sc, ls, lr,
+    st, sty, stm, stc, stx, sc, sd, pas, par, ls, lr,
     load_sem, pair_send, pair_recv,
     qa_send, qa_recv, qb_send, qb_recv, qy_send, qy_recv,
-    sty_send, sty_recv, stx_send, stx_recv, stm_send, stm_recv,
+    sty_send, sty_recv, stx_send, stx_recv, stm_send, stm_recv, pa_send, pa_recv,
     tb_send, tb_recv, ta_send, ta_recv, ty_send, ty_recv,
 ):
     g = lax.axis_index("qgrp")
@@ -227,6 +230,18 @@
     def stats_m(b):
         return rcopy(st.at[b], stm.at[b], stm_send.at[b], stm_recv.at[b], n3)
 
+    def peak_a(b):
+        return rcopy(pas.at[b], par.at[b], pa_send.at[b], pa_recv.at[b], n1)
+
+    def pair_scale(b):
+        stats_m(b).wait_recv()
+        here, there = st[b, 1:2, :], stm[b, 2:3, :]
+        peak = jnp.maximum(here, there)
+        sd[b, 0:1, :] = jnp.exp(here - peak)
+        sd[b, 1:2, :] = jnp.exp(there - peak)
+        pas[b] = jnp.broadcast_to(peak, (8, BATCH))
+        start(peak_a(b))
+
     def stats_x(b, i):
         dev = (n1, n2, n3)[i]
         return rcopy(stc.at[b], stx.at[b, i], stx_send.at[b, i], stx_recv.at[b, i], dev)
@@ -262,8 +277,8 @@
             log_totals.append(peak + jnp.log(total))
         for r in range(3):
             sc[b, r:r + 1, :] = jnp.exp(st[b, r:r + 1, :] - log_totals[r])
-        stats_m(b).wait_recv()
-        sc[b, 4:5, :] = jnp.exp(stm[b, 2:3, :] - log_totals[1])
+        peak_a(b).wait_recv()
+        sc[b, 4:5, :] = jnp.exp(par[b, 0:1, :] - log_totals[0])
         positive = own[6:7]
         sc[b, 3:4, :] = jnp.exp(positive - log_totals[0]) - 1.0
         loss = log_totals[0] - positive
@@ -304,7 +319,7 @@
             ev[1 + r, span, b * BATCH:(b + 1) * BATCH] = (e * scale).astype(BF16)
 
     def part(n):
-        return n % 2, pl.ds(HALF * (n // 2), HALF)
+        return n % 2, pl.ds(PART * (n // 2), PART)
 
     def tb(b, n):
         j, d = part(n)
@@ -334,14 +349,15 @@
         total = term(b, 2, i).astype(BF16)
         for j in range(2):
             sb[b, j, pl.ds(i * HALF, HALF), :] = total[:, lanes(j)]
-            start(tb(b, 2 * i + j))
+        for n in range(PARTS):
+            start(tb(b, PARTS * i + n))
 
     def send_a(b, n):
         j, d = part(n)
         tb(b, n).wait_recv()
         sa[b, j, d] = (
-            t1[b, d, lanes(j)] * sc[b, 1:2, lanes(j)]
-            + rb[b, j, d].astype(F32) * sc[b, 4:5, lanes(j)]
+            t1[b, d, lanes(j)] * sd[b, 0:1, lanes(j)]
+            + rb[b, j, d].astype(F32) * sd[b, 1:2, lanes(j)]
         ).astype(BF16)
         start(ta(b, n))
 
@@ -349,24 +365,25 @@
         j, d = part(n)
         unit = b + 2 * j
         ta(b, n).wait_recv()
+        total = t0[b, d, lanes(j)] + ra[b, j, d].astype(F32) * sc[b, 4:5, lanes(j)]
 
         @pl.when(y == unit)
         def _():
-            acc[d] = t0[b, d, lanes(j)] + ra[b, j, d].astype(F32)
+            acc[d] = total
 
         @pl.when(y != unit)
         def _():
-            sy[b, j, d] = (t0[b, d, lanes(j)] + ra[b, j, d].astype(F32)).astype(BF16)
+            sy[b, j, d] = total.astype(BF16)
             ty(b, n).start()
 
     def passage_part(half, i, target):
         total = None
         for r in range(3):
             add = dot_nn(
-                ev[r, pl.ds(half * SHARD + i * 512, 512), :], qv[r].reshape(QUERIES, D)
+                ev[r, pl.ds(half * SHARD + i * ROWS, ROWS), :], qv[r].reshape(QUERIES, D)
             )
             total = add if total is None else total + add
-        target[pl.ds(i * 512, 512), :] = total.astype(target.dtype)
+        target[pl.ds(i * ROWS, ROWS), :] = total.astype(target.dtype)
 
     def begin_stats(b):
         start(stats_m(b))
@@ -377,6 +394,14 @@
         combine_y(b)
         for i in range(3):
             start(stats_x(b, i))
+
+    def send_a_all(b, *pieces):
+        for n in pieces:
+            send_a(b, n)
+
+    def send_y_all(b, *pieces):
+        for n in pieces:
+            send_y(b, n)
 
     qy_wait(0, 0)
     lent(0, 0)
@@ -391,51 +416,65 @@
     forward_b(1, 2)
     send_b(0, 1)
     forward_b(1, 3)
+    terms(0, 1)
     begin_stats_x(0)
-    terms(0, 1)
+    pair_scale(0)
     qy_wait(1, 0)
     lent(1, 0)
-    combine_x(0)
-    send_a(0, 0)
+    send_a_all(0, 0, 1)
     qy_wait(1, 1)
     lent(1, 1)
     begin_stats(1)
-    send_a(0, 1)
+    send_a_all(0, 2)
     send_b(1, 0)
     send_b(1, 1)
-    send_a(0, 2)
+    send_a_all(0, 3, 4)
+    combine_x(0)
     own_weights(0)
     terms(0, 0)
-    send_a(0, 3)
+    send_a_all(0, 5, 6)
+    send_y_all(0, 0, 1, 2)
+    terms(1, 1)
+    send_a_all(0, 7)
+    send_y_all(0, 3, 4)
     begin_stats_x(1)
-    send_y(0, 0)
-    send_y(0, 1)
-    terms(1, 1)
+    pair_scale(1)
     lent_weights(0, 0)
     lent_weights(0, 1)
+    send_a_all(1, 0)
+    send_y_all(0, 5)
+    send_a_all(1, 1)
+    send_y_all(0, 6)
+    send_a_all(1, 2)
+    send_y_all(0, 7)
     combine_x(1)
     loss_copy = rcopy(ls, lr, pair_send.at[1], pair_recv.at[1], pair)
     start(loss_copy)
-    send_y(0, 2)
-    send_a(1, 0)
     own_weights(1)
     terms(1, 0)
-    send_a(1, 1)
-    send_y(0, 3)
+    send_a_all(1, 3, 4)
+    send_y_all(1, 0, 1)
     lent_weights(1, 0)
     lent_weights(1, 1)
     passage_part(1, 0, pgs)
-    send_a(1, 2)
     passage_part(1, 1, pgs)
+    send_a_all(1, 5)
+    send_y_all(1, 2)
+    send_a_all(1, 6)
+    send_y_all(1, 3)
+    passage_part(1, 2, pgs)
+    send_a_all(1, 7)
+    send_y_all(1, 4)
+    passage_part(1, 3, pgs)
     pg_copy = rcopy(pgs, pgr, pair_send.at[2], pair_recv.at[2], pair)
     start(pg_copy)
-    send_a(1, 3)
-    send_y(1, 0)
+    send_y_all(1, 5)
     passage_part(0, 0, pgo)
-    send_y(1, 1)
+    send_y_all(1, 6)
     passage_part(0, 1, pgo)
-    send_y(1, 2)
-    send_y(1, 3)
+    send_y_all(1, 7)
+    passage_part(0, 2, pgo)
+    passage_part(0, 3, pgo)
     loss_copy.wait_recv()
     for j in range(4):
         loss_ref[pl.ds(2 * j + c, 1), :] = ls[j:j + 1, :]
@@ -444,8 +483,8 @@
     for i in range(4):
         span = pl.ds(i * 256, 256)
         pg_ref[span, :] = (pgo[span, :] + pgr[span, :].astype(F32)).astype(BF16)
-    for i in range(2):
-        d = slice(i * HALF, (i + 1) * HALF)
+    for i in range(PARTS):
+        d = slice(i * PART, (i + 1) * PART)
         total = acc[d]
         for slot in range(3):
             rcopy(
@@ -456,7 +495,7 @@
     for copy in sends:
         copy.wait_send()
     for b in range(NB):
-        for n in range(4):
+        for n in range(2 * PARTS):
             @pl.when(y != b + 2 * (n % 2))
             def _():
                 ty(b, n).wait_send()
@@ -507,14 +546,17 @@
             vmem((NB, 8, BATCH), F32),
             vmem((NB, 3, 8, BATCH), F32),
             vmem((NB, 8, BATCH), F32),
+            vmem((NB, 8, BATCH), F32),
+            vmem((NB, 8, BATCH), F32),
+            vmem((NB, 8, BATCH), F32),
             vmem((8, UNIT), F32),
             vmem((8, UNIT), F32),
             dma((2 * NB + 1,)), dma((3,)), dma((3,)),
             dma((NB, PIECES)), dma((NB, PIECES)), dma((NB, PIECES)), dma((NB, PIECES)),
             dma((NB, 2, PIECES)), dma((NB, 2, PIECES)),
-            dma((NB, 3)), dma((NB, 3)), dma((NB, 3)), dma((NB, 3)), dma((NB,)), dma((NB,)),
-            dma((NB, 4)), dma((NB, 4)), dma((NB, 4)), dma((NB, 4)),
-            dma((NB, 4)), dma((3, 2)),
+            dma((NB, 3)), dma((NB, 3)), dma((NB, 3)), dma((NB, 3)), dma((NB,)), dma((NB,)), dma((NB,)), dma((NB,)),
+            dma((NB, 8)), dma((NB, 8)), dma((NB, 8)), dma((NB, 8)),
+            dma((NB, 8)), dma((3, PARTS)),
         ],
         compiler_params=pltpu.CompilerParams(
             collective_id=0, has_side_effects=True, vmem_limit_bytes=52 * 1024 * 1024

time: 74.3 us -> 67 us (0.902)
  Pallas kernels: 70.6 us -> 63.6 us
    pallas_call x1, Pallas kernels: 70.6 us -> 63.6 us  [on_device(): pl.pallas_call(kernel, out_shape=(pltpu.VMEM((8, 128), F32), pltpu.VMEM((...]
where the time goes in v4:
time: 67 us; the launch traced here: 66.8 us
  Pallas kernels  63.6 us (95%)
  local copies, waits for them, and re-layouts  2.62 us (4%)
    pallas_call x1, Pallas kernels, on_device(): pl.pallas_call(kernel, out_shape=(pltpu.VMEM((8, 128), F32), pltpu.VMEM((...  63.6 us
    unnamed x3, local copies, waits for them, and re-layouts  2.62 us

profile of v4, /device:TPU:24, one launch (start us, length us, event | category | flops | bytes accessed | tf_op | source)
XLA Modules:
  0.0 66.8 jit_solution(9589875374125759163)
XLA Ops:
  0.6 63.6 %shard_map.67 = (f32[8,128]{1,0:T(8,128)S(1)}, bf16[128,1024]{1,0:T(8,128)(2,1)S(1)}, bf16[1024,1024]{1,0:T(8,128)(2,1)S(1)}) custom-call(bf16[4,2,128,1024]{3,2,1,0:T(8,128)(2,1)} %bitcast.4, bf16[1024,1024]{1,0:T(8,128)(2,1)} %p_hbm.1, s32[2,16]{1,0:T(2,128)} %mask_ref.1, s32[8,128]{1,0:T(8,128)} %bitcast.5), custom_call_target="tpu_custom_call" | custom-call | flops 19327352832 | bytes 7340032 | tf_op jit(solution)/shard_map/pallas_call | solution.py:507
  64.2 0.6 copy.10
  64.8 0.7 %copy.11 = bf16[128,1024]{1,0:T(8,128)(2,1)} copy(bf16[128,1024]{1,0:T(8,128)(2,1)S(1)} %get-tuple-element.10) | data formatting | bytes 524288
  65.5 1.3 %copy.12 = bf16[1024,1024]{1,0:T(8,128)(2,1)} copy(bf16[1024,1024]{1,0:T(8,128)(2,1)S(1)} %get-tuple-element.11) | data formatting | bytes 4194304

commit v5 on v4

--- a/solution.py
+++ b/solution.py
@@ -21,6 +21,8 @@
 PARTS = 4
 PART = 256
 ROWS = 256
+LAST = D - PART
+CHAIN = 2 * PARTS - 2
 LOW = -1e30
 MESH = pl.DeviceIdType.MESH
 
@@ -36,14 +38,15 @@
 def kernel(
     q_hbm, p_hbm, mask_ref, pos_ref,
     loss_ref, qg_ref, pg_ref,
-    qv, pv, pt, lg, ev, t1, t0,
-    sb, rb, sa, ra, sy, ry, acc,
+    qv, pv, pt, lg, ev, t2, t1, t0,
+    sb, rb, sa, ra, sy, ry, acc, zs, zr, za, zb, zc,
     pgs, pgr, pgo,
-    st, sty, stm, stc, stx, sc, sd, pas, par, ls, lr,
+    st, sty, stm, stc, stx, sc, sd, sf, pas, par, ls, lr,
     load_sem, pair_send, pair_recv,
     qa_send, qa_recv, qb_send, qb_recv, qy_send, qy_recv,
     sty_send, sty_recv, stx_send, stx_recv, stm_send, stm_recv, pa_send, pa_recv,
     tb_send, tb_recv, ta_send, ta_recv, ty_send, ty_recv,
+    z_send, z_recv, zx_send, zx_recv,
 ):
     g = lax.axis_index("qgrp")
     k = lax.axis_index("pcol")
@@ -162,16 +165,13 @@
     own_max = own_logits(0, own_max)
     transpose(0)
     forward_a(0, 0)
-    forward_a(0, 1)
     p_swap.wait_recv()
     own_max = own_logits(1, own_max)
+    forward_a(0, 1)
     forward_a(0, 2)
+    transpose(1)
     forward_b(0, 0)
     forward_a(0, 3)
-    forward_b(0, 1)
-    transpose(1)
-    forward_a(1, 0)
-    forward_b(0, 2)
 
     positive_all = jnp.concatenate([positive_row(b) for b in range(NB)], axis=1)
 
@@ -195,9 +195,12 @@
 
     zero = jnp.zeros((1, QUERIES), F32)
     own_sums = own_exp(0, (zero, zero))
+    forward_b(0, 1)
+    forward_a(1, 0)
+    own_total, own_positive = own_exp(1, own_sums)
+    forward_b(0, 2)
     forward_a(1, 1)
     forward_b(0, 3)
-    own_total, own_positive = own_exp(1, own_sums)
     for b in range(NB):
         part = slice(b * BATCH, (b + 1) * BATCH)
         st[b, 0:1, :] = own_max[:, part]
@@ -279,6 +282,11 @@
             sc[b, r:r + 1, :] = jnp.exp(st[b, r:r + 1, :] - log_totals[r])
         peak_a(b).wait_recv()
         sc[b, 4:5, :] = jnp.exp(par[b, 0:1, :] - log_totals[0])
+        here = jnp.exp(own[1:2] - log_totals[1])
+        there = jnp.exp(three[2:3] - log_totals[1])
+        for j in range(2):
+            sf[b + 2 * j, 0:1, :] = here[:, j * UNIT:(j + 1) * UNIT]
+            sf[b + 2 * j, 1:2, :] = there[:, j * UNIT:(j + 1) * UNIT]
         positive = own[6:7]
         sc[b, 3:4, :] = jnp.exp(positive - log_totals[0]) - 1.0
         loss = log_totals[0] - positive
@@ -345,12 +353,17 @@
     def lanes(j):
         return slice(j * UNIT, (j + 1) * UNIT)
 
-    def send_b(b, i):
-        total = term(b, 2, i).astype(BF16)
+    def make_b(b, i):
+        total = term(b, 2, i)
+        count = min(LAST - i * HALF, HALF)
         for j in range(2):
-            sb[b, j, pl.ds(i * HALF, HALF), :] = total[:, lanes(j)]
-        for n in range(PARTS):
-            start(tb(b, PARTS * i + n))
+            sb[b, j, i * HALF:i * HALF + count, :] = total[:count, lanes(j)].astype(BF16)
+        if count < HALF:
+            t2[b] = total[count:, :]
+
+    def send_b(b, *pieces):
+        for n in pieces:
+            start(tb(b, n))
 
     def send_a(b, n):
         j, d = part(n)
@@ -364,8 +377,10 @@
     def send_y(b, n):
         j, d = part(n)
         unit = b + 2 * j
-        ta(b, n).wait_recv()
-        total = t0[b, d, lanes(j)] + ra[b, j, d].astype(F32) * sc[b, 4:5, lanes(j)]
+        total = t0[b, d, lanes(j)]
+        if n < CHAIN:
+            ta(b, n).wait_recv()
+            total = total + ra[b, j, d].astype(F32) * sc[b, 4:5, lanes(j)]
 
         @pl.when(y == unit)
         def _():
@@ -375,6 +390,50 @@
         def _():
             sy[b, j, d] = total.astype(BF16)
             ty(b, n).start()
+
+    def ty_first(b, r, j):
+        unit = b + 2 * j
+        slot = lax.rem(y - unit + 4, 4) - 1
+        return rcopy(
+            zs.at[r, b, j], zr.at[r, slot], z_send.at[r, b, j], z_recv.at[r, slot],
+            (g, 2 * unit + c),
+        )
+
+    def first_y(b):
+        for r in (1, 0):
+            scale = jnp.exp(st[b, 1 + r:2 + r, :] - stc[b, 1 + r:2 + r, :])
+            total = (t1[b, LAST:, :] if r == 0 else t2[b]) * scale
+            for j in range(2):
+                @pl.when(y == b + 2 * j)
+                def _():
+                    za[r] = total[:, lanes(j)]
+
+                @pl.when(y != b + 2 * j)
+                def _():
+                    zs[r, b, j] = total[:, lanes(j)].astype(BF16)
+                    ty_first(b, r, j).start()
+
+    def first_sum(r):
+        total = za[r]
+        for slot in range(3):
+            rcopy(
+                zs.at[r, 0, 0], zr.at[r, slot], z_send.at[r, 0, 0], z_recv.at[r, slot], up
+            ).wait_recv()
+            total = total + zr[r, slot].astype(F32)
+        return total
+
+    zx_b = rcopy(zb.at[0], zc.at[0], zx_send.at[0], zx_recv.at[0], n3)
+    zx_a = rcopy(zb.at[1], zc.at[1], zx_send.at[1], zx_recv.at[1], n1)
+
+    def first_b():
+        zb[0] = first_sum(1).astype(BF16)
+        start(zx_b)
+
+    def first_a():
+        total = first_sum(0) * sf[y, 0:1, :]
+        zx_b.wait_recv()
+        zb[1] = (total + zc[0].astype(F32) * sf[y, 1:2, :]).astype(BF16)
+        start(zx_a)
 
     def passage_part(half, i, target):
         total = None
@@ -403,76 +462,76 @@
         for n in pieces:
             send_y(b, n)
 
+    forward_a(1, 2)
     qy_wait(0, 0)
     lent(0, 0)
-    forward_a(1, 2)
     forward_b(1, 0)
     forward_a(1, 3)
     forward_b(1, 1)
     qy_wait(0, 1)
     lent(0, 1)
     begin_stats(0)
-    send_b(0, 0)
+    make_b(0, 0)
+    send_b(0, 0, 1, 2, 3)
     forward_b(1, 2)
-    send_b(0, 1)
+    make_b(0, 1)
     forward_b(1, 3)
     terms(0, 1)
-    begin_stats_x(0)
-    pair_scale(0)
     qy_wait(1, 0)
     lent(1, 0)
-    send_a_all(0, 0, 1)
+    begin_stats_x(0)
+    send_b(0, 4, 5)
+    pair_scale(0)
+    send_a_all(0, 0)
+    first_y(0)
     qy_wait(1, 1)
     lent(1, 1)
     begin_stats(1)
-    send_a_all(0, 2)
-    send_b(1, 0)
-    send_b(1, 1)
-    send_a_all(0, 3, 4)
+    make_b(1, 0)
+    send_b(1, 0, 1)
+    send_a_all(0, 1, 2, 3)
+    make_b(1, 1)
+    send_a_all(0, 4)
     combine_x(0)
+    send_a_all(0, 5)
     own_weights(0)
     terms(0, 0)
-    send_a_all(0, 5, 6)
-    send_y_all(0, 0, 1, 2)
+    begin_stats_x(1)
+    send_b(1, 2, 3, 4, 5)
+    pair_scale(1)
+    send_y_all(0, 0, 1, 2, 3)
     terms(1, 1)
-    send_a_all(0, 7)
-    send_y_all(0, 3, 4)
-    begin_stats_x(1)
-    pair_scale(1)
+    first_y(1)
+    send_a_all(1, 0)
+    send_y_all(0, 4, 5, 6, 7)
+    send_a_all(1, 1)
     lent_weights(0, 0)
     lent_weights(0, 1)
-    send_a_all(1, 0)
-    send_y_all(0, 5)
-    send_a_all(1, 1)
-    send_y_all(0, 6)
     send_a_all(1, 2)
-    send_y_all(0, 7)
+    first_b()
     combine_x(1)
     loss_copy = rcopy(ls, lr, pair_send.at[1], pair_recv.at[1], pair)
     start(loss_copy)
     own_weights(1)
+    send_a_all(1, 3)
     terms(1, 0)
-    send_a_all(1, 3, 4)
-    send_y_all(1, 0, 1)
+    send_a_all(1, 4, 5)
+    send_y_all(1, 6, 7, 0, 1)
     lent_weights(1, 0)
     lent_weights(1, 1)
     passage_part(1, 0, pgs)
+    send_y_all(1, 2)
+    first_a()
     passage_part(1, 1, pgs)
-    send_a_all(1, 5)
-    send_y_all(1, 2)
-    send_a_all(1, 6)
     send_y_all(1, 3)
     passage_part(1, 2, pgs)
-    send_a_all(1, 7)
     send_y_all(1, 4)
+    send_y_all(1, 5)
     passage_part(1, 3, pgs)
     pg_copy = rcopy(pgs, pgr, pair_send.at[2], pair_recv.at[2], pair)
     start(pg_copy)
-    send_y_all(1, 5)
     passage_part(0, 0, pgo)
-    send_y_all(1, 6)
     passage_part(0, 1, pgo)
-    send_y_all(1, 7)
     passage_part(0, 2, pgo)
     passage_part(0, 3, pgo)
     loss_copy.wait_recv()
@@ -491,6 +550,9 @@
                 sy.at[0, 0, d], ry.at[slot, d], ty_send.at[0, 0], ty_recv.at[slot, i], up
             ).wait_recv()
             total = total + ry[slot, d].astype(F32)
+        if i == PARTS - 1:
+            zx_a.wait_recv()
+            total = total + zc[1].astype(F32)
         qg_ref[:, d] = total.T.astype(BF16)
     for copy in sends:
         copy.wait_send()
@@ -499,6 +561,11 @@
             @pl.when(y != b + 2 * (n % 2))
             def _():
                 ty(b, n).wait_send()
+        for j in range(2):
+            @pl.when(y != b + 2 * j)
+            def _():
+                for r in range(2):
+                    ty_first(b, r, j).wait_send()
 
 
 def on_device(queries, passages, block_mask, positives):
@@ -528,6 +595,7 @@
             vmem((D, CHIP), BF16),
             vmem((CHIP, QUERIES), F32),
             vmem((3, CHIP, QUERIES), BF16),
+            vmem((NB, PART, BATCH), F32),
             vmem((NB, D, BATCH), F32),
             vmem((NB, D, BATCH), F32),
             vmem((NB, 2, D, UNIT), BF16),
@@ -537,6 +605,11 @@
             vmem((NB, 2, D, UNIT), BF16),
             vmem((3, D, UNIT), BF16),
             vmem((D, UNIT), F32),
+            vmem((2, NB, 2, PART, UNIT), BF16),
+            vmem((2, 3, PART, UNIT), BF16),
+            vmem((2, PART, UNIT), F32),
+            vmem((2, PART, UNIT), BF16),
+            vmem((2, PART, UNIT), BF16),
             vmem((SHARD, D), BF16),
             vmem((SHARD, D), BF16),
             vmem((SHARD, D), F32),
@@ -547,6 +620,7 @@
             vmem((NB, 3, 8, BATCH), F32),
             vmem((NB, 8, BATCH), F32),
             vmem((NB, 8, BATCH), F32),
+            vmem((4, 8, UNIT), F32),
             vmem((NB, 8, BATCH), F32),
             vmem((NB, 8, BATCH), F32),
             vmem((8, UNIT), F32),
@@ -557,6 +631,7 @@
             dma((NB, 3)), dma((NB, 3)), dma((NB, 3)), dma((NB, 3)), dma((NB,)), dma((NB,)), dma((NB,)), dma((NB,)),
             dma((NB, 8)), dma((NB, 8)), dma((NB, 8)), dma((NB, 8)),
             dma((NB, 8)), dma((3, PARTS)),
+            dma((2, NB, 2)), dma((2, 3)), dma((2,)), dma((2,)),
         ],
         compiler_params=pltpu.CompilerParams(
             collective_id=0, has_side_effects=True, vmem_limit_bytes=52 * 1024 * 1024

time: 67 us -> 62.8 us (0.937)
  the two profiles are of different devices: /device:TPU:24 before, /device:TPU:9 now
where the time goes in v5:
time: 62.8 us; the launch traced here: 62.6 us
  Pallas kernels  59.4 us (95%)
  local copies, waits for them, and re-layouts  2.62 us (4%)
  between operations  0.64 us (1%)
    pallas_call x1, Pallas kernels, on_device(): pl.pallas_call(kernel, out_shape=(pltpu.VMEM((8, 128), F32), pltpu.VMEM((...  59.4 us
    unnamed x3, local copies, waits for them, and re-layouts  2.62 us

profile of v5, /device:TPU:9, one launch (start us, length us, event | category | flops | bytes accessed | tf_op | source)
XLA Modules:
  0.0 62.6 jit_solution(16246814205193069452)
XLA Ops:
  0.6 59.4 %shard_map.67 = (f32[8,128]{1,0:T(8,128)S(1)}, bf16[128,1024]{1,0:T(8,128)(2,1)S(1)}, bf16[1024,1024]{1,0:T(8,128)(2,1)S(1)}) custom-call(bf16[4,2,128,1024]{3,2,1,0:T(8,128)(2,1)} %bitcast.4, bf16[1024,1024]{1,0:T(8,128)(2,1)} %p_hbm.1, s32[2,16]{1,0:T(2,128)} %mask_ref.1, s32[8,128]{1,0:T(8,128)} %bitcast.5), custom_call_target="tpu_custom_call" | custom-call | flops 19327352832 | bytes 7340032 | tf_op jit(solution)/shard_map/pallas_call | solution.py:574
  60.0 0.6 copy.10
  60.6 0.7 %copy.11 = bf16[128,1024]{1,0:T(8,128)(2,1)} copy(bf16[128,1024]{1,0:T(8,128)(2,1)S(1)} %get-tuple-element.10) | data formatting | bytes 524288
  61.3 1.3 %copy.12 = bf16[1024,1024]{1,0:T(8,128)(2,1)} copy(bf16[1024,1024]{1,0:T(8,128)(2,1)S(1)} %get-tuple-element.11) | data formatting | bytes 4194304
